TPU v7x, 128 devices: a whole 4x4x4 slice. The times are simulated.
128 devices in a mesh: rows: 8 (over y, core), keys: 16 (over z, x).
Axes of the slice: x: 4, y: 4, z: 4, core: 2. Of those that a mesh axis runs over, the one named last changes fastest.
Arguments:
- pair_rep: bfloat16 [512, 512, 128], P('rows', 'keys'), may hold values from -6 to 6
- token_mask: int32 [512], replicated, may hold values from 0 to 1, as said below
- norm_gain: float32 [2, 128], replicated, may hold values from 0.5 to 1.5
- norm_shift: float32 [2, 128], replicated, may hold values from -0.5 to 0.5
- w_proj: bfloat16 [2, 128, 512], replicated, may hold values from -1 to 1
- w_bias: bfloat16 [2, 128, 4], replicated, may hold values from -0.25 to 0.25
- gate_bias: float32 [2, 128], replicated, may hold values from -1.5 to 1.5
- w_out: bfloat16 [2, 128, 128], replicated, may hold values from -0.5 to 0.5
Outputs:
- new_pair: bfloat16 [512, 512, 128], P('rows', 'keys')
Inputs may be any that keep to these rules, and one draw needn't show every extreme that they name: token_mask is 1 on a leading run of at least 256 tokens and 0 on the rest, with at least one 0.
All inputs are finite; a program needn't handle non-finite values.
Results may differ from a plain program's by a relative error of at most 0.02.
Values may be sent and summed in bfloat16 or wider, within the bound.
A program may use at most 128 MiB of HBM per device.

v0:
```python
import jax
import jax.numpy as jnp
from jax import lax
from jax.sharding import PartitionSpec as P


def spread_2(x, axis, root):
    mine = lax.axis_index(axis) == root
    return lax.psum(jnp.where(mine, x, jnp.zeros_like(x)), axis)


def layer_norm(values, norm_gain, norm_shift):
    center = jnp.mean(values, axis=-1, keepdims=True)
    spread = jnp.mean((values - center) ** 2, axis=-1, keepdims=True)
    return (values - center) * lax.rsqrt(spread + 1e-05) * norm_gain + norm_shift


def swap_along_keys(blocks):
    return lax.all_to_all(blocks, "keys", split_axis=0, concat_axis=0, tiled=True)


def swap_along_rows(blocks):
    return lax.all_to_all(blocks, "rows", split_axis=0, concat_axis=0, tiled=True)


def to_columns(pair_tile):
    rows_n, cols_n, channels = pair_tile.shape
    key_count = lax.axis_size("keys")
    row_count = lax.axis_size("rows")
    group_size = key_count // row_count
    piece_rows = rows_n // key_count
    moved = swap_along_keys(pair_tile.reshape(key_count, piece_rows, cols_n, channels))
    spread_rows = moved.transpose(1, 0, 2, 3).reshape(
        piece_rows, row_count, row_count, group_size, piece_rows, channels
    )
    arranged = spread_rows.transpose(2, 3, 1, 4, 0, 5).reshape(
        row_count, rows_n, piece_rows, channels
    )
    moved_back = swap_along_rows(arranged)
    return moved_back.transpose(1, 0, 2, 3).reshape(rows_n, cols_n, channels)


def to_rows(pair_tile):
    rows_n, cols_n, channels = pair_tile.shape
    key_count = lax.axis_size("keys")
    row_count = lax.axis_size("rows")
    group_size = key_count // row_count
    piece_rows = rows_n // key_count
    arranged = pair_tile.reshape(rows_n, row_count, piece_rows, channels).transpose(1, 0, 2, 3)
    moved = swap_along_rows(arranged)
    spread_rows = moved.reshape(row_count, group_size, row_count, piece_rows, piece_rows, channels)
    full_rows = spread_rows.transpose(4, 2, 0, 1, 3, 5).reshape(
        piece_rows, key_count, cols_n, channels
    )
    moved_back = swap_along_keys(full_rows.transpose(1, 0, 2, 3))
    return moved_back.reshape(rows_n, cols_n, channels)


def local_pass(
    pair_tile, key_bias, gain_vec, shift_vec, w_proj_one, w_bias_one, gate_bias_one, w_out_one
):
    rows_n, cols_n, channels = pair_tile.shape
    key_count = lax.axis_size("keys")
    group_size = key_count // lax.axis_size("rows")
    hidden_width = w_out_one.shape[0]
    head_count = w_bias_one.shape[1]
    head_size = hidden_width // head_count
    row_block = 8
    normed = layer_norm(pair_tile.astype(jnp.float32), gain_vec, shift_vec).astype(jnp.bfloat16)
    flat_rows = normed.reshape(rows_n * cols_n, channels)
    projected = jnp.dot(flat_rows, w_proj_one, preferred_element_type=jnp.float32)
    queries = (
        (projected[:, :hidden_width] * head_size ** (-0.5))
        .astype(jnp.bfloat16)
        .reshape(rows_n, cols_n, head_count, head_size)
    )
    key_value = (
        projected[:, hidden_width : 3 * hidden_width]
        .astype(jnp.bfloat16)
        .reshape(rows_n, cols_n, 2 * hidden_width)
    )
    gating = jax.nn.sigmoid(projected[:, 3 * hidden_width :] + gate_bias_one)
    tile_bias = jnp.dot(flat_rows, w_bias_one, preferred_element_type=jnp.float32).astype(
        jnp.bfloat16
    )
    tile_bias = tile_bias.reshape(rows_n, cols_n, head_count).transpose(2, 0, 1)
    start_carry = (
        jnp.full((rows_n, cols_n, head_count), -1e30, jnp.float32),
        jnp.zeros((rows_n, cols_n, head_count), jnp.float32),
        jnp.zeros((rows_n, cols_n, head_count, head_size), jnp.float32),
    )
    row_bias = lax.all_gather(tile_bias, "keys", axis=2, tiled=True)
    own_rows = lax.dynamic_slice_in_dim(
        row_bias, lax.axis_index("keys") % group_size * cols_n, cols_n, 1
    )
    query_bias = spread_2(own_rows, "rows", lax.axis_index("keys") // group_size).transpose(1, 0, 2)
    key_tile = lax.all_gather(key_value, "keys", axis=1, tiled=True)
    count_keys = key_tile.shape[1]
    score_bias = query_bias.astype(jnp.float32) + key_bias
    key_part = key_tile[..., :hidden_width].reshape(rows_n, count_keys, head_count, head_size)
    value_part = key_tile[..., hidden_width:].reshape(rows_n, count_keys, head_count, head_size)

    def absorb_block(operands):
        query_rows, key_rows, value_rows, running_max, running_sum, running_out = operands
        scores = (
            jnp.einsum("ijhd,ikhd->ijhk", query_rows, key_rows, preferred_element_type=jnp.float32)
            + score_bias
        )
        new_max = jnp.maximum(running_max, jnp.max(scores, axis=-1))
        expo = jnp.exp(scores - new_max[..., None])
        rescale = jnp.exp(running_max - new_max)
        new_sum = running_sum * rescale + jnp.sum(expo, axis=-1)
        added = jnp.einsum(
            "ijhk,ikhd->ijhd",
            expo.astype(jnp.bfloat16),
            value_rows,
            preferred_element_type=jnp.float32,
        )
        return (new_max, new_sum, running_out * rescale[..., None] + added)

    block_count = rows_n // row_block
    stacked = tuple(
        (
            item.reshape((block_count, row_block) + item.shape[1:])
            for item in (queries, key_part, value_part) + tuple(start_carry)
        )
    )
    results = lax.map(absorb_block, stacked)
    final_carry = tuple((item.reshape((rows_n,) + item.shape[2:]) for item in results))
    attended = final_carry[2] / final_carry[1][..., None]
    gated = (attended.reshape(rows_n * cols_n, hidden_width) * gating).astype(jnp.bfloat16)
    return jnp.dot(gated, w_out_one, preferred_element_type=jnp.float32).reshape(
        rows_n, cols_n, channels
    )


def local(pair_rep, token_mask, norm_gain, norm_shift, w_proj, w_bias, gate_bias, w_out):
    mask_float = token_mask.astype(jnp.float32)
    key_bias = (mask_float - 1.0) * 1000000000.0
    token_total = token_mask.shape[0]
    rows_n, cols_n, _ = pair_rep.shape
    row_mask = lax.dynamic_slice_in_dim(mask_float, lax.axis_index("rows") * rows_n, rows_n, 0)
    col_mask = lax.dynamic_slice_in_dim(mask_float, lax.axis_index("keys") * cols_n, cols_n, 0)
    pair_mask = (row_mask[:, None] * col_mask[None, :])[..., None]
    start_branch = local_pass(
        pair_rep,
        key_bias,
        norm_gain[0],
        norm_shift[0],
        w_proj[0],
        w_bias[0],
        gate_bias[0],
        w_out[0],
    )
    after_start = (pair_rep.astype(jnp.float32) + pair_mask * start_branch).astype(jnp.bfloat16)
    turned = to_columns(after_start)
    permuted_bias = (
        key_bias.reshape(lax.axis_size("rows"), lax.axis_size("keys"), -1)
        .transpose(1, 0, 2)
        .reshape(token_total)
    )
    ending = local_pass(
        turned,
        permuted_bias,
        norm_gain[1],
        norm_shift[1],
        w_proj[1],
        w_bias[1],
        gate_bias[1],
        w_out[1],
    )
    end_update = to_rows(ending.astype(jnp.bfloat16))
    masked_end = pair_mask * end_update.astype(jnp.float32)
    return (after_start.astype(jnp.float32) + masked_end).astype(jnp.bfloat16)


def solution(mesh):
    in_specs = (P("rows", "keys", None), P(), P(), P(), P(), P(), P(), P())
    out_specs = P("rows", "keys", None)
    return jax.shard_map(local, mesh=mesh, in_specs=in_specs, out_specs=out_specs, check_vma=False)
```

profile of v0, /device:TPU:1, one launch (start us, length us, event | category | flops | bytes accessed | tf_op | source)
XLA Modules:
  0.0 580.7 jit_solution(8937026757823554851)
XLA Ops:
  14.1 21.0 %all_gather.13 = bf16[4,64,512]{1,0,2:T(4,128)(2,1)S(1)} all-gather(bf16[4,64,32]{1,0,2:T(4,128)(2,1)S(1)} %copy.56), channel_id=1, replica_groups=mesh['rows'=8,'keys'=16] {'keys'}, dimensions={2}, use_global_device_ids=true | all-gather | bytes 278528 | tf_op jit(solution)/shard_map/all_gather | solution.py:92
  37.1 2.0 copy-done
  41.6 1.8 reshape_reshape.19
  44.1 56.4 %all-reduce.3.cloned.1.call-done = bf16[4,32,512]{1,0,2:T(4,128)(2,1)} async-done(((bf16[4,32,512]{1,0,2:T(4,128)(2,1)}), bf16[4,32,512]{1,0,2:T(4,128)(2,1)}) %all-reduce.3.cloned.1.call-update) | async-done | bytes 131088 | tf_op jit(solution)/shard_map/psum | solution.py:9
  102.6 53.6 %all-gather.3.cloned.1.call-done = bf16[64,512,256]{2,1,0:T(8,128)(2,1)} async-done(((bf16[64,32,256]{2,1,0:T(8,128)(2,1)}), bf16[64,512,256]{2,1,0:T(8,128)(2,1)}) %all-gather.3.cloned.1.call-update) | async-done | bytes 16777232 | tf_op jit(solution)/shard_map/all_gather | solution.py:97
  156.2 11.6 %fusion.74 = (bf16[64,512,128]{2,1,0:T(8,128)(2,1)}, bf16[64,512,128]{2,1,0:T(8,128)(2,1)}) fusion(bf16[64,512,256]{2,1,0:T(8,128)(2,1)} %all-gather.3.cloned.1.call-done), kind=kLoop, calls=%fused_computation.123 | loop fusion | bytes 33554432 | tf_op jit(solution)/shard_map/slice | solution.py:101
  167.7 12.0 %copy.55 = bf16[64,512,128]{1,2,0:T(8,128)(2,1)} copy(bf16[64,512,128]{2,1,0:T(8,128)(2,1)} %get-tuple-element.180) | data formatting | bytes 16777216 | tf_op jit(solution)/shard_map/slice | solution.py:100
  179.7 11.9 %copy.57 = bf16[64,512,128]{1,2,0:T(8,128)(2,1)} copy(bf16[64,512,128]{2,1,0:T(8,128)(2,1)} %get-tuple-element.179) | data formatting | bytes 16777216 | tf_op jit(solution)/shard_map/slice | solution.py:101
  191.6 3.0 broadcast.224.clone2
  195.3 55.0 %while.24 = (s32[]{:T(128)}, f32[8,8,32,4]{2,3,1,0:T(4,128)}, f32[8,8,32,4,32]{4,3,2,1,0:T(4,128)}, bf16[8,8,512,4,32]{2,4,3,1,0:T(8,128)(2,1)}, bf16[8,8,32,4,3...) while((s32[]{:T(128)}, f32[8,8,32,4]{2,3,1,0:T(4,128)}, ...), condition=%wide.region_6.7_spmd, body=%wide.region_3.6_spmd.sunk | while | flops 71341056 | bytes 10479705 | solution.py:128
  198.1 1.8 fusion.95
  204.9 1.8 fusion.95
  210.1 1.7 fusion.93
  211.8 1.8 fusion.95
  218.7 1.8 fusion.95
  225.6 1.8 fusion.95
  232.5 1.8 fusion.95
  239.4 1.8 fusion.95
  246.2 1.8 fusion.95
  251.2 2.5 div.59
  253.7 3.6 div.60
  257.7 3.8 reshape.250
  263.5 15.6 %all_to_all.20 = bf16[16,4,32,128]{3,2,1,0:T(8,128)(2,1)S(1)} all-to-all(bf16[16,4,32,128]{3,2,1,0:T(8,128)(2,1)S(1)} %bitcast.212), channel_id=1, replica_groups=mesh['rows'=8,'keys'=16] {'keys'}, dimensions={0} | all-to-all | bytes 1048576 | tf_op jit(solution)/shard_map/all_to_all | solution.py:19
  279.5 15.4 %all_to_all.21 = bf16[8,64,4,128]{3,2,1,0:T(4,128)(2,1)S(1)} all-to-all(bf16[8,64,4,128]{3,2,1,0:T(4,128)(2,1)S(1)} %copy.65), channel_id=1, replica_groups=mesh['rows'=8,'keys'=16] {'rows'}, dimensions={0} | all-to-all | bytes 1048576 | tf_op jit(solution)/shard_map/all_to_all | solution.py:23
  298.8 16.6 %all_gather.15 = bf16[4,64,512]{1,0,2:T(4,128)(2,1)S(1)} all-gather(bf16[4,64,32]{1,0,2:T(4,128)(2,1)S(1)} %copy.68), channel_id=1, replica_groups=mesh['rows'=8,'keys'=16] {'keys'}, dimensions={2}, use_global_device_ids=true | all-gather | bytes 278528 | tf_op jit(solution)/shard_map/all_gather | solution.py:92
  317.4 2.0 copy-done.1
  322.1 1.8 reshape_reshape.22
  323.9 55.1 %all-reduce.5.cloned.1.call-done = bf16[4,32,512]{1,0,2:T(4,128)(2,1)} async-done(((bf16[4,32,512]{1,0,2:T(4,128)(2,1)}), bf16[4,32,512]{1,0,2:T(4,128)(2,1)}) %all-reduce.5.cloned.1.call-update) | async-done | bytes 131088 | tf_op jit(solution)/shard_map/psum | solution.py:9
  381.0 53.6 %all-gather.5.cloned.1.call-done = bf16[64,512,256]{2,1,0:T(8,128)(2,1)} async-done(((bf16[64,32,256]{2,1,0:T(8,128)(2,1)}), bf16[64,512,256]{2,1,0:T(8,128)(2,1)}) %all-gather.5.cloned.1.call-update) | async-done | bytes 16777232 | tf_op jit(solution)/shard_map/all_gather | solution.py:97
  434.5 11.6 %fusion.73 = (bf16[64,512,128]{2,1,0:T(8,128)(2,1)}, bf16[64,512,128]{2,1,0:T(8,128)(2,1)}) fusion(bf16[64,512,256]{2,1,0:T(8,128)(2,1)} %all-gather.5.cloned.1.call-done), kind=kLoop, calls=%fused_computation.122 | loop fusion | bytes 33554432 | tf_op jit(solution)/shard_map/slice | solution.py:101
  446.1 12.0 %copy.67 = bf16[64,512,128]{1,2,0:T(8,128)(2,1)} copy(bf16[64,512,128]{2,1,0:T(8,128)(2,1)} %get-tuple-element.178) | data formatting | bytes 16777216 | tf_op jit(solution)/shard_map/slice | solution.py:100
  458.1 11.9 %copy.70 = bf16[64,512,128]{1,2,0:T(8,128)(2,1)} copy(bf16[64,512,128]{2,1,0:T(8,128)(2,1)} %get-tuple-element.177) | data formatting | bytes 16777216 | tf_op jit(solution)/shard_map/slice | solution.py:101
  470.0 3.0 broadcast.224.clone
  473.6 55.0 %while.25 = (s32[]{:T(128)}, f32[8,8,32,4]{2,3,1,0:T(4,128)}, f32[8,8,32,4,32]{4,3,2,1,0:T(4,128)}, bf16[8,8,512,4,32]{2,4,3,1,0:T(8,128)(2,1)}, bf16[8,8,32,4,3...) while((s32[]{:T(128)}, f32[8,8,32,4]{2,3,1,0:T(4,128)}, ...), condition=%wide.region_13.14_spmd, body=%wide.region_10.13_spmd.sunk | while | flops 71341056 | bytes 10479705 | solution.py:128
  476.4 1.8 fusion.100
  483.3 1.8 fusion.100
  490.2 1.8 fusion.100
  497.1 1.8 fusion.100
  502.2 1.8 fusion.98
  504.0 1.8 fusion.100
  510.8 1.8 fusion.100
  517.7 1.8 fusion.100
  524.6 1.8 fusion.100
  529.5 2.5 div.66
  532.0 3.6 div.67
  536.0 3.7 reshape.257
  541.9 14.2 %all_to_all.22 = bf16[8,64,4,128]{3,2,1,0:T(4,128)(2,1)S(1)} all-to-all(bf16[8,64,4,128]{3,2,1,0:T(4,128)(2,1)S(1)} %bitcast.223), channel_id=1, replica_groups=mesh['rows'=8,'keys'=16] {'rows'}, dimensions={0} | all-to-all | bytes 1048576 | tf_op jit(solution)/shard_map/all_to_all | solution.py:23
  557.0 15.1 %all_to_all.23 = bf16[16,4,32,128]{3,2,1,0:T(8,128)(2,1)S(1)} all-to-all(bf16[16,4,32,128]{3,2,1,0:T(8,128)(2,1)S(1)} %copy.79), channel_id=1, replica_groups=mesh['rows'=8,'keys'=16] {'keys'}, dimensions={0} | all-to-all | bytes 1048576 | tf_op jit(solution)/shard_map/all_to_all | solution.py:19
  (197 shorter events, 112.4 us)
Async XLA Ops:
  7.4 29.0 %copy-start.5 = (bf16[2,128,512]{2,1,0:T(8,128)(2,1)S(1)}, bf16[2,128,512]{2,1,0:T(8,128)(2,1)}, u32[]{:S(2)}) copy-start(bf16[2,128,512]{2,1,0:T(8,128)(2,1)} %param.16) | copy-start | bytes 786436
  7.4 93.2 %all-reduce.3.cloned.1.call-start = ((), (), s32[]{:S(2)}) async-start(), calls=%async_computation.5 | async-start | bytes 1048576 | tf_op jit(solution)/shard_map/psum | solution.py:9
  36.3 119.9 %all-gather.3.cloned.1.call-start = ((), (), s32[]{:S(2)}) async-start(), calls=%async_computation.4 | async-start | bytes 17825792 | tf_op jit(solution)/shard_map/all_gather | solution.py:97
  37.0 2.1 copy-start
  39.1 4.3 copy-start.8
  39.1 4.5 copy-start.11
  40.2 338.7 %all-reduce.5.cloned.1.call-start = ((), (), s32[]{:S(2)}) async-start(), calls=%async_computation.7 | async-start | bytes 1048576 | tf_op jit(solution)/shard_map/psum | solution.py:9
  257.3 4.2 copy-start.10
  257.7 5.5 copy-start.2
  257.7 5.5 copy-start.7
  263.5 15.7 %copy-start.3 = (bf16[64,32,128]{2,1,0:T(8,128)(2,1)}, bf16[64,32,128]{2,1,0:T(8,128)(2,1)S(1)}, u32[]{:S(2)}) copy-start(bf16[64,32,128]{2,1,0:T(8,128)(2,1)S(1)} %fusion.30) | copy-start | bytes 1572868
  279.2 19.2 %copy-start.9 = (bf16[2,128,4]{1,2,0:T(4,128)(2,1)S(1)}, bf16[2,128,4]{1,2,0:T(4,128)(2,1)}, u32[]{:S(2)}) copy-start(bf16[2,128,4]{1,2,0:T(4,128)(2,1)} %param.17) | copy-start | bytes 6148
  294.9 21.8 %copy-start.6 = (bf16[2,128,512]{2,1,0:T(8,128)(2,1)S(1)}, bf16[2,128,512]{2,1,0:T(8,128)(2,1)}, u32[]{:S(2)}) copy-start(bf16[2,128,512]{2,1,0:T(8,128)(2,1)} %param.16) | copy-start | bytes 786436
  316.6 117.9 %all-gather.5.cloned.1.call-start = ((), (), s32[]{:S(2)}) async-start(), calls=%async_computation.6 | async-start | bytes 17825792 | tf_op jit(solution)/shard_map/all_gather | solution.py:97
  317.4 2.1 copy-start.1
  541.4 30.8 %copy-start.4 = (bf16[64,32,128]{2,1,0:T(8,128)(2,1)S(1)}, bf16[64,32,128]{2,1,0:T(8,128)(2,1)}, u32[]{:S(2)}) copy-start(bf16[64,32,128]{2,1,0:T(8,128)(2,1)} %copy-done.3) | copy-start | bytes 1572868
Sparse Core Ops, SparseCore 0:
  36.4 64.1 all-reduce.2
  316.7 62.1 all-reduce.4
Sparse Core Ops, SparseCore 1:
  40.3 115.8 all-gather.2
  320.6 113.8 all-gather.4
where the time goes:
time: 585 us; the launch traced here: 581 us
  waiting for transfers between devices  219 us (37%)
  local copies, waits for them, and re-layouts  149 us (25%)
  blocking collectives  97.8 us (17%)
  matrix products  59.1 us (10%)
  other arithmetic  40.5 us (7%)
  between operations  15.3 us (3%)
    psum x2, waiting for transfers between devices, spread_2(): return lax.psum(jnp.where(mine, x, jnp.zeros_like(x)), axis)  111 us
    all_gather x2, waiting for transfers between devices, local_pass(): key_tile = lax.all_gather(key_value, 'keys', axis=1, tiled=True)  107 us
    slice x4, local copies, waits for them, and re-layouts, local_pass(): key_tile[..., hidden_width:]  47 us
    all_gather x2, blocking collectives, local_pass(): row_bias = lax.all_gather(tile_bias, 'keys', axis=2, tiled=True)  37.6 us
    all_to_all x2, blocking collectives, swap_along_keys(): lax.all_to_all(blocks, 'keys', split_axis=0, concat_axis=0, tiled=True)  30.7 us
    all_to_all x2, blocking collectives, swap_along_rows(): lax.all_to_all(blocks, 'rows', split_axis=0, concat_axis=0, tiled=True)  29.6 us
    dot_general x16, matrix products, absorb_block(): jnp.einsum('ijhk,ikhd->ijhd', expo.astype(jnp.bfloat16), value_rows, pref...  28.3 us
    dot_general x16, matrix products, absorb_block(): jnp.einsum('ijhd,ikhd->ijhk', query_rows, key_rows, preferred_element_typ...  27.6 us
  transfers between devices with their start and end apart: 4, of which 4 were waited for; matrix products, arithmetic and copies ran while one was open for 3% of the time, Pallas kernels for 0%

commit v1 on v0

v1 whole, which is shorter than its diff:
```python
import functools

import jax
import jax.numpy as jnp
from jax import lax
from jax.experimental import pallas as pl
from jax.experimental.pallas import tpu as pltpu
from jax.sharding import PartitionSpec as P

MESH = pl.DeviceIdType.MESH
LOG2E = 1.4426950408889634
F32 = jnp.float32
BF16 = jnp.bfloat16
KEYS = 32
HEADS = 4
HEAD = 32
LANES = 128
CHUNK = 256


def layer_norm(values, gain, shift):
    center = jnp.mean(values, axis=-1, keepdims=True)
    moved = values - center
    spread = jnp.mean(moved * moved, axis=-1, keepdims=True)
    return moved * lax.rsqrt(spread + 1e-05) * gain + shift


def head_max(m, lane):
    for step in (16, 8, 4, 2, 1):
        below = pltpu.roll(m, step, 1)
        above = pltpu.roll(m, LANES - step, 1)
        m = jnp.maximum(m, jnp.where((lane & step) != 0, below, above))
    return m


def kernel(
    tokens, row_n, key_n,
    x_ref, kb_ref, mk_ref, gain_ref, shift_ref, wp_ref, wb_ref, gb_ref, wo_ref,
    out_ref,
    x1, x2, as1, np2, t2, sb, fin, tile_f, bias_a, bias_b, bias_s, q_s, k_s, v_s, g_s, s_s,
    a1_send, a1_recv, a2_send, a2_recv, b2_send, b2_recv, c2_send, c2_recv,
    ga_send, ga_recv, gb_send, gb_recv,
):
    rows_t, cols_t = tokens // row_n, tokens // key_n
    per = tokens // (row_n * key_n)
    groups = tokens // KEYS
    y_n = row_n // 2
    z_n = x_n = int(round(key_n**0.5))
    y_h = y_n // 2
    r, c = lax.axis_index("rows"), lax.axis_index("keys")
    y, core = r // 2, r % 2
    z, xx = c // x_n, c % x_n
    lane = lax.broadcasted_iota(jnp.int32, (1, LANES), 1)

    barrier = pltpu.get_barrier_semaphore()

    def greet_keys(o, carry):
        pl.semaphore_signal(barrier, inc=1, device_id=(r, lax.rem(c + o, key_n)), device_id_type=MESH)
        return carry

    def greet_rows(o, carry):
        pl.semaphore_signal(barrier, inc=1, device_id=(lax.rem(r + o, row_n), c), device_id_type=MESH)
        return carry

    lax.fori_loop(1, key_n, greet_keys, 0)
    lax.fori_loop(1, row_n, greet_rows, 0)

    lane_k = lax.broadcasted_iota(jnp.int32, (LANES, LANES), 1)
    sub_k = lax.broadcasted_iota(jnp.int32, (LANES, LANES), 0)
    ones = jnp.where(lane_k // HEAD == sub_k // KEYS, 1.0, 0.0).astype(BF16)

    def put_ones(i, carry):
        for g in range(groups):
            v_s[i, g * LANES : (g + 1) * LANES, LANES:] = ones
        return carry

    lax.fori_loop(0, per, put_ones, 0)
    pl.semaphore_wait(barrier, key_n - 1 + row_n - 1)

    def remote(src, dst, send, recv, device):
        return pltpu.make_async_remote_copy(
            src_ref=src, dst_ref=dst, send_sem=send, recv_sem=recv,
            device_id=device, device_id_type=MESH,
        )

    def col_slice(which):
        return pl.ds(pl.multiple_of(which * cols_t, cols_t), cols_t)

    def row_slice(which):
        return pl.ds(pl.multiple_of(which * rows_t, rows_t), rows_t)

    def send_a1(o, carry):
        to = lax.rem(c + o, key_n)
        remote(x_ref.at[pl.ds(to * per, per)], x1.at[:, col_slice(c)], a1_send.at[o], a1_recv.at[o], (r, to)).start()
        return carry

    def wait_a1(o, carry):
        to = lax.rem(c + key_n - o, key_n)
        copy = remote(x_ref.at[pl.ds(to * per, per)], x1.at[:, col_slice(to)], a1_send.at[o], a1_recv.at[o], (r, to))
        copy.wait_send()
        copy.wait_recv()
        return carry

    def gather_start(buf, send, recv):
        sends = []
        for d in range(1, y_n):
            to = lax.rem(y + d, y_n)
            own = buf.at[y, core, z, xx]
            copy = remote(own, own, send.at[d], recv.at[d], (to * 2 + core, c))
            copy.start()
            sends.append(copy)
        return sends

    def gather_plan(buf, send, recv):
        base = y_n
        n1 = z_n - 1
        mate = (y * 2 + 1 - core, c)

        def zdev(d):
            return (r, lax.rem(z + d, z_n) * x_n + xx)

        def xdev(d):
            return (r, z * x_n + lax.rem(xx + d, x_n))

        def zoff(d):
            return lax.rem(z + z_n - d, z_n)

        def xoff(d):
            return lax.rem(xx + x_n - d, x_n)

        low, high = slice(0, y_h), slice(y_h, y_n)
        s1_in = [remote(buf.at[lax.rem(y + y_n - d, y_n), core, z, xx], buf.at[lax.rem(y + y_n - d, y_n), core, z, xx],
                        send.at[d], recv.at[d], (lax.rem(y + y_n - d, y_n) * 2 + core, c)) for d in range(1, y_n)]
        s2_out, s2_in, s3_out, s3_in = [], [], [], []
        m2, m3 = [], []

        def both(ref, slot, device, outs):
            outs.append(remote(ref, ref, send.at[slot], recv.at[slot], device))

        slot = base
        for d in range(1, z_n):
            both(buf.at[low, core, z, xx], slot, zdev(d), s2_out)
            both(buf.at[low, core, zoff(d), xx], slot, zdev(z_n - d), s2_in)
            slot += 1
            both(buf.at[high, core, z, xx], slot, xdev(d), s2_out)
            both(buf.at[high, core, z, xoff(d)], slot, xdev(x_n - d), s2_in)
            slot += 1
        for d in range(1, z_n):
            both(buf.at[low, core, :, xx], slot, xdev(d), s3_out)
            both(buf.at[low, core, :, xoff(d)], slot, xdev(x_n - d), s3_in)
            slot += 1
            both(buf.at[high, core, z, :], slot, zdev(d), s3_out)
            both(buf.at[high, core, zoff(d), :], slot, zdev(z_n - d), s3_in)
            slot += 1
        m_out, m_in = [], []
        both(buf.at[:, core, z, xx], slot, mate, m_out)
        both(buf.at[:, 1 - core, z, xx], slot, mate, m_in)
        slot += 1
        for d in range(1, z_n):
            both(buf.at[low, core, zoff(d), xx], slot, mate, m_out)
            both(buf.at[low, 1 - core, zoff(d), xx], slot, mate, m_in)
            slot += 1
            both(buf.at[high, core, z, xoff(d)], slot, mate, m_out)
            both(buf.at[high, 1 - core, z, xoff(d)], slot, mate, m_in)
            slot += 1
        for d in range(1, z_n):
            both(buf.at[low, core, :, xoff(d)], slot, mate, m_out)
            both(buf.at[low, 1 - core, :, xoff(d)], slot, mate, m_in)
            slot += 1
            both(buf.at[high, core, zoff(d), :], slot, mate, m_out)
            both(buf.at[high, 1 - core, zoff(d), :], slot, mate, m_in)
            slot += 1
        return s1_in, s2_out, s2_in, s3_out, s3_in, m_out, m_in

    def start_all(copies):
        for copy in copies:
            copy.start()

    lane_q = lax.broadcasted_iota(jnp.int32, (KEYS, LANES), 1)

    def prepare(m, xs, i):
        normed = layer_norm(xs[i].astype(F32), gain_ref[m], shift_ref[m]).astype(BF16)

        def project(part):
            return jnp.dot(normed, wp_ref[m, :, part * LANES : (part + 1) * LANES], preferred_element_type=F32)

        q_s[i] = (project(0) * HEAD**-0.5).astype(BF16)
        k = project(1).astype(BF16)
        v = project(2).astype(BF16)
        g_s[i] = jax.nn.sigmoid(project(3) + gb_ref[m])
        for g in range(groups):
            kg = k[g * KEYS : (g + 1) * KEYS]
            vg = v[g * KEYS : (g + 1) * KEYS]
            for h in range(HEADS):
                mine = lane_q // HEAD == h
                at = g * LANES + h * KEYS
                k_s[i, at : at + KEYS, :] = jnp.where(mine, kg, jnp.zeros_like(kg))
                v_s[i, at : at + KEYS, :LANES] = jnp.where(mine, vg, jnp.zeros_like(vg))

    def attend(m, i):
        width = groups * LANES
        q = q_s[i]
        top = None
        for n in range(0, width, CHUNK):
            s = lax.dot_general(q, k_s[i, n : n + CHUNK, :], (((1,), (1,)), ((), ())), preferred_element_type=F32)
            s = s + bias_s[:, n : n + CHUNK]
            s_s[:, n : n + CHUNK] = s
            for t in range(0, CHUNK, LANES):
                part = s[:, t : t + LANES]
                top = part if top is None else jnp.maximum(top, part)
        top = head_max(top, lane)
        top = jnp.concatenate([top] * (CHUNK // LANES), axis=1)
        total = jnp.zeros((tokens, 2 * LANES), F32)
        for n in range(0, width, CHUNK):
            p = jnp.exp2((s_s[:, n : n + CHUNK] - top) * LOG2E).astype(BF16)
            total = total + jnp.dot(p, v_s[i, n : n + CHUNK, :], preferred_element_type=F32)
        gated = (total[:, :LANES] / total[:, LANES:] * g_s[i]).astype(BF16)
        return jnp.dot(gated, wo_ref[m], preferred_element_type=F32)

    lax.fori_loop(1, key_n, send_a1, 0)
    x1[:, col_slice(c)] = x_ref[pl.ds(c * per, per)]

    tile_f[...] = layer_norm(x_ref[...].astype(F32), gain_ref[0], shift_ref[0])

    def pick(m, k):
        return jnp.where(lane_k % KEYS == k, wb_ref[m], jnp.zeros((LANES, LANES), BF16))

    acc = jnp.zeros((rows_t, LANES), F32)
    for k in range(0, cols_t, 2):
        left = jnp.concatenate([tile_f[:, k, :], tile_f[:, k + 1, :]], axis=1).astype(BF16)
        right = jnp.concatenate([pick(0, k), pick(0, k + 1)], axis=0)
        acc = acc + jnp.dot(left, right, preferred_element_type=F32)
    bias_a[y, core, z, xx] = acc.astype(BF16)

    def run_gather(buf, send, recv, work):
        s1_out = gather_start(buf, send, recv)
        s1_in, s2_out, s2_in, s3_out, s3_in, m_out, m_in = gather_plan(buf, send, recv)
        n1 = 2 * (z_n - 1)
        for copy in s1_in:
            copy.wait_recv()
        start_all(s2_out)
        m_out[0].start()
        work[0]()
        for copy in s2_in:
            copy.wait_recv()
        start_all(s3_out)
        start_all(m_out[1 : 1 + n1])
        work[1]()
        for arrived, onward in zip(s3_in, m_out[1 + n1 :]):
            arrived.wait_recv()
            onward.start()
        work[2]()
        for copy in m_in:
            copy.wait_recv()
        for copy in s1_out + s2_out + s3_out + m_out:
            copy.wait_send()

    def first_rows():
        lax.fori_loop(1, key_n, wait_a1, 0)
        prepare(0, x1, 0)

    def more(m, xs, lo, hi):
        def one(i, carry):
            prepare(m, xs, i)
            return carry

        lax.fori_loop(lo, hi, one, 0)

    run_gather(bias_a, ga_send, ga_recv, [first_rows, lambda: more(0, x1, 1, per), lambda: None])

    for yy in range(y_n):
        for cc in range(2):
            def widen(g, carry, yy=yy, cc=cc):
                at = pl.ds(pl.multiple_of(g * LANES, LANES), LANES)
                block = bias_a[yy, cc, g // x_n, g % x_n].astype(F32)
                rr = yy * 2 + cc
                bias_s[rr * rows_t : (rr + 1) * rows_t, at] = block + kb_ref[pl.ds(g, 1), :]
                return carry

            lax.fori_loop(0, key_n, widen, 0)

    def a2_copy(i, n, o, to, frm):
        return remote(
            as1.at[pl.ds(i, n), col_slice(to)], t2.at[pl.ds(frm * per + i, n)], a2_send.at[o], a2_recv.at[o], (r, to)
        )

    def row_one(i, carry):
        update = attend(0, i)
        keep = mk_ref[pl.ds(rows_t * r + per * c + i, 1), :] * mk_ref[...]
        as1[i] = (x1[i].astype(F32) + keep * update).astype(BF16)

        def send(o, inner):
            to = lax.rem(c + o, key_n)
            a2_copy(i, 1, o, to, c).start()
            return inner

        lax.fori_loop(1, key_n, send, 0)
        t2[per * c + i] = as1[i, col_slice(c)]
        return carry

    lax.fori_loop(0, per, row_one, 0)

    def wait_a2(o, carry):
        a2_copy(0, per, o, lax.rem(c + o, key_n), c).wait_send()
        frm = lax.rem(c + key_n - o, key_n)
        a2_copy(0, per, o, frm, frm).wait_recv()
        return carry

    lax.fori_loop(1, key_n, wait_a2, 0)

    tile_f[...] = t2[...].astype(F32)
    for j in range(cols_t):
        sb[j] = tile_f[:, j, :].astype(BF16)

    def b2_copy(o, to, frm):
        return remote(sb.at[pl.ds(to * per, per)], x2.at[:, row_slice(frm)], b2_send.at[o], b2_recv.at[o], (to, c))

    def send_b2(o, carry):
        b2_copy(o, lax.rem(r + o, row_n), r).start()
        return carry

    def wait_b2(o, carry):
        b2_copy(o, lax.rem(r + o, row_n), r).wait_send()
        frm = lax.rem(r + row_n - o, row_n)
        b2_copy(o, frm, frm).wait_recv()
        return carry

    lax.fori_loop(1, row_n, send_b2, 0)
    x2[:, row_slice(r)] = sb[pl.ds(r * per, per)]

    tile_f[...] = layer_norm(tile_f[...], gain_ref[1], shift_ref[1])
    halves = rows_t // KEYS

    acc = jnp.zeros((rows_t, LANES), F32)
    for k in range(0, KEYS, 2):
        left = jnp.concatenate(
            [jnp.concatenate([tile_f[h * KEYS + kk] for h in range(halves)], axis=0) for kk in (k, k + 1)], axis=1
        ).astype(BF16)
        right = jnp.concatenate([pick(1, k), pick(1, k + 1)], axis=0)
        acc = acc + jnp.dot(left, right, preferred_element_type=F32)
    bias_b[y, core, z, xx] = acc.astype(BF16)

    def second_rows():
        lax.fori_loop(1, row_n, wait_b2, 0)
        prepare(1, x2, 0)

    run_gather(bias_b, gb_send, gb_recv, [second_rows, lambda: more(1, x2, 1, per), lambda: None])

    for yy in range(y_n):
        for cc in range(2):
            for h in range(halves):
                def widen_two(g, carry, yy=yy, cc=cc, h=h):
                    lane_at = ((yy * 2 + cc) * halves + h)
                    block = bias_b[yy, cc, g // x_n, g % x_n, h * KEYS : (h + 1) * KEYS, :].astype(F32)
                    bias_s[col_slice(g), lane_at * LANES : (lane_at + 1) * LANES] = (
                        block + kb_ref[lane_at : lane_at + 1, :]
                    )
                    return carry

                lax.fori_loop(0, key_n, widen_two, 0)

    def c2_copy(i, n, o, to, frm):
        return remote(
            np2.at[pl.ds(i, n), row_slice(to)], fin.at[pl.ds(frm * per + i, n)], c2_send.at[o], c2_recv.at[o], (to, c)
        )

    def row_two(i, carry):
        update = attend(1, i)
        keep = mk_ref[pl.ds(cols_t * c + per * r + i, 1), :] * mk_ref[...]
        update = (keep * update).astype(BF16).astype(F32)
        np2[i] = (x2[i].astype(F32) + update).astype(BF16)

        def send(o, inner):
            c2_copy(i, 1, o, lax.rem(r + o, row_n), r).start()
            return inner

        lax.fori_loop(1, row_n, send, 0)
        fin[per * r + i] = np2[i, row_slice(r)]
        return carry

    lax.fori_loop(0, per, row_two, 0)

    def wait_c2(o, carry):
        c2_copy(0, per, o, lax.rem(r + o, row_n), r).wait_send()
        frm = lax.rem(r + row_n - o, row_n)
        c2_copy(0, per, o, frm, frm).wait_recv()
        return carry

    lax.fori_loop(1, row_n, wait_c2, 0)
    for j in range(cols_t):
        tile_f[:, j, :] = fin[j].astype(F32)
    out_ref[...] = tile_f[...].astype(BF16)


def local(row_n, key_n, pair_rep, token_mask, norm_gain, norm_shift, w_proj, w_bias, gate_bias, w_out):
    rows_t, cols_t, channels = pair_rep.shape
    tokens = token_mask.shape[0]
    per = tokens // (row_n * key_n)
    groups = tokens // KEYS
    width = groups * LANES
    mask = token_mask.astype(F32)
    key_bias = (mask - 1.0) * 1000000000.0
    kb = jnp.tile(key_bias.reshape(groups, 1, KEYS), (1, HEADS, 1)).reshape(groups, LANES)
    mk = jnp.broadcast_to(mask[:, None], (tokens, LANES))
    wb = jnp.repeat(w_bias, KEYS, axis=2)
    y_n, z_n = row_n // 2, int(round(key_n**0.5))
    slots = y_n + 4 * (z_n - 1) + 1 + 4 * (z_n - 1)
    vmem, dma = pltpu.VMEM, pltpu.SemaphoreType.DMA
    buf = (y_n, 2, z_n, z_n, rows_t, LANES)
    return pl.pallas_call(
        functools.partial(kernel, tokens, row_n, key_n),
        out_shape=jax.ShapeDtypeStruct(pair_rep.shape, BF16),
        in_specs=[pl.BlockSpec(memory_space=pltpu.VMEM)] * 9,
        out_specs=pl.BlockSpec(memory_space=pltpu.VMEM),
        scratch_shapes=[
            vmem((per, tokens, LANES), BF16),
            vmem((per, tokens, LANES), BF16),
            vmem((per, tokens, LANES), BF16),
            vmem((per, tokens, LANES), BF16),
            vmem((rows_t, cols_t, LANES), BF16),
            vmem((cols_t, rows_t, LANES), BF16),
            vmem((cols_t, rows_t, LANES), BF16),
            vmem((rows_t, cols_t, LANES), F32),
            vmem(buf, BF16),
            vmem(buf, BF16),
            vmem((tokens, width), F32),
            vmem((per, tokens, LANES), BF16),
            vmem((per, width, LANES), BF16),
            vmem((per, width, 2 * LANES), BF16),
            vmem((per, tokens, LANES), F32),
            vmem((tokens, width), F32),
            dma((key_n,)), dma((key_n,)), dma((key_n,)), dma((key_n,)),
            dma((row_n,)), dma((row_n,)), dma((row_n,)), dma((row_n,)),
            dma((slots,)), dma((slots,)), dma((slots,)), dma((slots,)),
        ],
        compiler_params=pltpu.CompilerParams(
            collective_id=0, has_side_effects=True, vmem_limit_bytes=56 * 2**20
        ),
        name="triangle_attention",
    )(
        pair_rep, kb, mk, norm_gain[:, None, :], norm_shift[:, None, :], w_proj, wb,
        gate_bias[:, None, :], w_out,
    )


def solution(mesh):
    row_n, key_n = mesh.shape["rows"], mesh.shape["keys"]
    in_specs = (P("rows", "keys", None), P(), P(), P(), P(), P(), P(), P())
    out_specs = P("rows", "keys", None)
    return jax.shard_map(
        functools.partial(local, row_n, key_n), mesh=mesh, in_specs=in_specs, out_specs=out_specs, check_vma=False
    )
```

time: 585 us -> 101 us (0.17)
  waiting for transfers between devices: 219 us -> 0 us
  local copies, waits for them, and re-layouts: 149 us -> 4.9 us
  blocking collectives: 97.8 us -> 0 us
  Pallas kernels: 0 us -> 95.4 us
  matrix products: 59.1 us -> 0 us
  other arithmetic: 40.5 us -> 0.01 us
  between operations: 15.3 us -> 0.02 us
    psum x2 -> x0, waiting for transfers between devices: 111 us -> none  [spread_2(): return lax.psum(jnp.where(mine, x, jnp.zeros_like(x)), axis)]
    all_gather x2 -> x0, waiting for transfers between devices: 107 us -> none  [local_pass(): key_tile = lax.all_gather(key_value, 'keys', axis=1, tiled=True)]
    pallas_call x0 -> x1, Pallas kernels: none -> 95.4 us  [local(): pl.pallas_call(functools.partial(kernel, tokens, row_n, key_n), out_shape...]
    slice x8 -> x0, local copies, waits for them, and re-layouts: 73.2 us -> none  [the longest x4 47 us: local_pass(): key_tile[..., hidden_width:]]
    all_to_all x4 -> x0, blocking collectives: 60.2 us -> none  [the longest x2 30.7 us: swap_along_keys(): lax.all_to_all(blocks, 'keys', split_axis=0, concat_axis=0, tiled=True)]
    dot_general x38 -> x0, matrix products: 59.1 us -> none  [the longest x16 28.3 us: absorb_block(): jnp.einsum('ijhk,ikhd->ijhd', expo.astype(jnp.bfloat16), value_rows, pref...]
    all_gather x2 -> x0, blocking collectives: 37.6 us -> none  [local_pass(): row_bias = lax.all_gather(tile_bias, 'keys', axis=2, tiled=True)]
    dynamic_update_slice x32 -> x0, local copies, waits for them, and re-layouts: 17.2 us -> none  [local_pass(): results = lax.map(absorb_block, stacked)]
  transfers between devices with their start and end apart: 4 -> 0, of which waited for: 4 -> 0; matrix products, arithmetic and copies ran while one was open for 3% -> 0% of each run, Pallas kernels for 0% -> 0%
where the time goes in v1:
time: 101 us; the launch traced here: 100 us
  Pallas kernels  95.4 us (94%)
  local copies, waits for them, and re-layouts  4.9 us (5%)
    pallas_call x1, Pallas kernels, local(): pl.pallas_call(functools.partial(kernel, tokens, row_n, key_n), out_shape...  95.4 us
    unnamed x5, local copies, waits for them, and re-layouts  2.56 us

profile of v1, /device:TPU:1, one launch (start us, length us, event | category | flops | bytes accessed | tf_op | source)
XLA Modules:
  0.0 100.4 jit_solution(9225882542016758424)
XLA Ops:
  0.0 0.0 copy-start
  0.0 0.7 copy-done
  0.7 0.1 tile.9
  0.8 0.0 copy-start.1
  0.8 0.7 tile.11.kb_ref
  1.5 0.0 copy-done.1
  1.5 0.7 copy.10.wb_ref
  2.2 0.8 broadcast_in_dim.18.mk_ref
  3.0 95.4 %triangle_attention.1 = bf16[64,32,128]{2,1,0:T(8,128)(2,1)} custom-call(bf16[64,32,128]{2,1,0:T(8,128)(2,1)} %x_ref.1, f32[16,128]{1,0:T(8,128)} %tile.11.kb_ref, f32[512,128]{1,0:T(8,128)} %broadcast_in_dim.18.mk_ref, f32[2,1,128]{2,1,0:T(1,128)} %bitcast.7, f32[2,1,128]{2,1,0:T(1,128)} %bitcast.8, bf16[2,128,512]{2,1,0:T(8,128)(2,1)} %wp_ref.1, ...), custom_call_target="tpu_custom_call" | custom-call | tf_op jit(solution)/shard_map/triangle_attention/pallas_call | solution.py:410
  98.5 1.9 %copy.12 = bf16[64,32,128]{2,1,0:T(8,128)(2,1)} copy(bf16[64,32,128]{2,1,0:T(8,128)(2,1)} %triangle_attention.1) | data formatting | bytes 1048576
  (4 shorter events, 0.0 us)
Async XLA Ops:
  0.0 0.7 copy-start
  0.8 0.7 copy-start.1

commit v2 on v1

v2 whole, which is shorter than its diff:
```python
import functools

import jax
import jax.numpy as jnp
from jax import lax
from jax.experimental import pallas as pl
from jax.experimental.pallas import tpu as pltpu
from jax.sharding import PartitionSpec as P

MESH = pl.DeviceIdType.MESH
LOG2E = 1.4426950408889634
F32 = jnp.float32
BF16 = jnp.bfloat16
KEYS = 32
HEADS = 4
HEAD = 32
LANES = 128
CHUNK = 256


def layer_norm(values, gain, shift):
    center = jnp.mean(values, axis=-1, keepdims=True)
    moved = values - center
    spread = jnp.mean(moved * moved, axis=-1, keepdims=True)
    return moved * lax.rsqrt(spread + 1e-05) * gain + shift


def head_max(m, lane):
    for step in (16, 8, 4, 2, 1):
        below = pltpu.roll(m, step, 1)
        above = pltpu.roll(m, LANES - step, 1)
        m = jnp.maximum(m, jnp.where((lane & step) != 0, below, above))
    return m


def kernel(
    tokens, row_n, key_n,
    x_ref, mask_ref, gain_ref, shift_ref, wp_ref, wb_ref, gb_ref, wo_ref,
    out_ref,
    x1, x2, as1, np2, t2, sb, fin, tile_f, bias_a, bias_b, bias_s, q_s, k_s, v_s, g_s,
    s_even, s_odd, p_even, p_odd, top_s, wr_s,
    a1_send, a1_recv, a2_send, a2_recv, b2_send, b2_recv, c2_send, c2_recv,
    ga_send, ga_recv, gb_send, gb_recv,
):
    rows_t, cols_t = tokens // row_n, tokens // key_n
    per = tokens // (row_n * key_n)
    groups = tokens // KEYS
    y_n = row_n // 2
    z_n = x_n = int(round(key_n**0.5))
    half_t = tokens // 2
    r, c = lax.axis_index("rows"), lax.axis_index("keys")
    y, core = r // 2, r % 2
    z, xx = c // x_n, c % x_n
    lane = lax.broadcasted_iota(jnp.int32, (1, LANES), 1)

    barrier = pltpu.get_barrier_semaphore()

    def greet_keys(o, carry):
        pl.semaphore_signal(barrier, inc=1, device_id=(r, lax.rem(c + o, key_n)), device_id_type=MESH)
        return carry

    def greet_rows(o, carry):
        pl.semaphore_signal(barrier, inc=1, device_id=(lax.rem(r + o, row_n), c), device_id_type=MESH)
        return carry

    lax.fori_loop(1, key_n, greet_keys, 0)
    lax.fori_loop(1, row_n, greet_rows, 0)

    real = jnp.sum(mask_ref[...], keepdims=True)

    def key_bias(g):
        key = g * KEYS + lane % KEYS
        return jnp.where(key < real, 0.0, -1000000000.0)

    def kept(first, token, count):
        at = first + lax.broadcasted_iota(jnp.int32, (count, LANES), 0)
        return jnp.where(jnp.logical_and(at < real, token < real), 1.0, 0.0)

    lane_k = lax.broadcasted_iota(jnp.int32, (LANES, LANES), 1)
    sub_k = lax.broadcasted_iota(jnp.int32, (LANES, LANES), 0)
    ones = jnp.where(lane_k // HEAD == sub_k // KEYS, 1.0, 0.0).astype(BF16)

    def put_ones(i, carry):
        for g in range(groups):
            v_s[i, g * LANES : (g + 1) * LANES, LANES:] = ones
        return carry

    lax.fori_loop(0, per, put_ones, 0)
    spread = lax.broadcasted_iota(jnp.int32, (HEADS, LANES), 0) == lax.broadcasted_iota(jnp.int32, (HEADS, LANES), 1) // KEYS
    spread = jnp.where(spread, 1.0, 0.0).astype(BF16)
    for m in range(2):
        wr_s[m] = jnp.dot(wb_ref[m], spread, preferred_element_type=F32).astype(BF16)
    pl.semaphore_wait(barrier, key_n - 1 + row_n - 1)

    def remote(src, dst, send, recv, device):
        return pltpu.make_async_remote_copy(
            src_ref=src, dst_ref=dst, send_sem=send, recv_sem=recv,
            device_id=device, device_id_type=MESH,
        )

    def col_slice(which):
        return pl.ds(pl.multiple_of(which * cols_t, cols_t), cols_t)

    def row_slice(which):
        return pl.ds(pl.multiple_of(which * rows_t, rows_t), rows_t)

    def send_a1(o, carry):
        to = lax.rem(c + o, key_n)
        remote(x_ref.at[pl.ds(to * per, per)], x1.at[:, col_slice(c)], a1_send.at[o], a1_recv.at[o], (r, to)).start()
        return carry

    def wait_a1(o, carry):
        to = lax.rem(c + key_n - o, key_n)
        copy = remote(x_ref.at[pl.ds(to * per, per)], x1.at[:, col_slice(to)], a1_send.at[o], a1_recv.at[o], (r, to))
        copy.wait_send()
        copy.wait_recv()
        return carry

    size = {"y": y_n, "z": z_n, "x": x_n}
    place = {"y": y, "z": z, "x": xx}

    def device(which_core, **at):
        at = {**place, **at}
        return (at["y"] * 2 + which_core, at["z"] * x_n + at["x"])

    def shifted(axis, d):
        return lax.rem(place[axis] + d, size[axis])

    class Gather:
        def __init__(self, buf, send, recv, axes):
            self.buf, self.send, self.recv = buf, send, recv
            self.first, self.others = axes[0], axes[1:]
            self.parts = size[axes[0]]
            self.turns = size[axes[1]] - 1

        def block(self, which_core, **at):
            at = {**place, **at}
            return self.buf.at[at["y"], which_core, at["z"], at["x"]]

        def copy(self, slot, ref, to):
            return remote(ref, ref, self.send.at[slot], self.recv.at[slot], to)

        def line(self, p, which_core, **at):
            u, v = self.others if p % 2 == 0 else self.others[::-1]
            return self.block(which_core, **{self.first: p, u: slice(None), v: at.get("v", place[v])})

        def one(self, d, out):
            near = shifted(self.first, size[self.first] - d)
            if out:
                return self.copy(d - 1, self.block(core), device(core, **{self.first: shifted(self.first, d)}))
            return self.copy(d - 1, self.block(core, **{self.first: near}), device(core, **{self.first: near}))

        def two(self, p, d, out):
            u = self.others[p % 2]
            slot = self.parts - 1 + p * self.turns + d - 1
            near = shifted(u, size[u] - d)
            if out:
                return self.copy(slot, self.block(core, **{self.first: p}), device(core, **{u: shifted(u, d)}))
            return self.copy(slot, self.block(core, **{self.first: p, u: near}), device(core, **{u: near}))

        def three(self, p, d, out):
            v = self.others[1 - p % 2]
            slot = self.parts - 1 + (self.parts + p) * self.turns + d - 1
            near = shifted(v, size[v] - d)
            if out:
                return self.copy(slot, self.line(p, core), device(core, **{v: shifted(v, d)}))
            return self.copy(slot, self.line(p, core, v=near), device(core, **{v: near}))

        def mate(self, p, d, out):
            v = self.others[1 - p % 2]
            slot = self.parts - 1 + 2 * self.parts * self.turns + p * (self.turns + 1) + d
            near = shifted(v, size[v] - d)
            return self.copy(slot, self.line(p, core if out else 1 - core, v=near), device(1 - core))

        def steps(self):
            return range(1, self.turns + 1)

        def start_one(self):
            for d in range(1, self.parts):
                self.one(d, True).start()

        def start_two(self):
            for d in range(1, self.parts):
                self.one(d, False).wait_recv()
            for p in range(self.parts):
                for d in self.steps():
                    self.two(p, d, True).start()

        def half(self, h):
            return range(h * self.parts // 2, (h + 1) * self.parts // 2)

        def start_three(self, h):
            for p in self.half(h):
                for d in self.steps():
                    self.two(p, d, False).wait_recv()
                for d in self.steps():
                    self.three(p, d, True).start()
                self.mate(p, 0, True).start()

        def pass_on(self, h):
            for d in self.steps():
                for p in self.half(h):
                    self.three(p, d, False).wait_recv()
                    self.mate(p, d, True).start()

        def finish(self, h):
            for p in self.half(h):
                for d in range(self.turns + 1):
                    self.mate(p, d, False).wait_recv()

        def drain(self):
            for d in range(1, self.parts):
                self.one(d, True).wait_send()
            for p in range(self.parts):
                for d in self.steps():
                    self.two(p, d, True).wait_send()
                    self.three(p, d, True).wait_send()
                for d in range(self.turns + 1):
                    self.mate(p, d, True).wait_send()

    lane_q = lax.broadcasted_iota(jnp.int32, (KEYS, LANES), 1)

    def prepare(m, xs, i):
        normed = layer_norm(xs[i].astype(F32), gain_ref[m : m + 1], shift_ref[m : m + 1]).astype(BF16)

        def project(part):
            return jnp.dot(normed, wp_ref[m, :, part * LANES : (part + 1) * LANES], preferred_element_type=F32)

        q_s[i] = (project(0) * HEAD**-0.5).astype(BF16)
        k = project(1).astype(BF16)
        v = project(2).astype(BF16)
        g_s[i] = jax.nn.sigmoid(project(3) + gb_ref[m : m + 1])
        for g in range(groups):
            kg = k[g * KEYS : (g + 1) * KEYS]
            vg = v[g * KEYS : (g + 1) * KEYS]
            for h in range(HEADS):
                mine = lane_q // HEAD == h
                at = g * LANES + h * KEYS
                k_s[i, at : at + KEYS, :] = jnp.where(mine, kg, jnp.zeros_like(kg))
                v_s[i, at : at + KEYS, :LANES] = jnp.where(mine, vg, jnp.zeros_like(vg))

    width = groups * LANES

    def score_chunk(row, at, s_s, n, top):
        s = lax.dot_general(
            q_s[row, at, :], k_s[row, n : n + CHUNK, :], (((1,), (1,)), ((), ())), preferred_element_type=F32
        )
        s = s + bias_s[at, n : n + CHUNK]
        s_s[:, n : n + CHUNK] = s
        for t in range(0, CHUNK, LANES):
            part = s[:, t : t + LANES]
            top = part if top is None else jnp.maximum(top, part)
        return top

    def weight_chunk(s_s, p_s, n, top):
        p_s[:, n : n + CHUNK] = jnp.exp2((s_s[:, n : n + CHUNK] - top) * LOG2E).astype(BF16)

    def attend(m, unit_done, between):
        units = 2 * per

        def where(unit):
            return lax.rem(unit, per), pl.ds(pl.multiple_of(unit // per * half_t, half_t), half_t)

        def scores(unit, s_s, slot, before=None):
            row, at = where(unit)
            top = None
            if before is not None:
                s_b, p_b, slot_b = before
                top_b = jnp.concatenate([top_s[slot_b]] * (CHUNK // LANES), axis=1)
            for n in range(0, width, CHUNK):
                if before is not None:
                    weight_chunk(s_b, p_b, n, top_b)
                top = score_chunk(row, at, s_s, n, top)
            top_s[slot] = head_max(top, lane)

        def weights(s_s, p_s, slot):
            top = jnp.concatenate([top_s[slot]] * (CHUNK // LANES), axis=1)
            for n in range(0, width, CHUNK):
                weight_chunk(s_s, p_s, n, top)

        def values(unit, p_s):
            row, at = where(unit)
            total = jnp.dot(p_s[...], v_s[row], preferred_element_type=F32)
            gated = (total[:, :LANES] / total[:, LANES:] * g_s[row, at, :]).astype(BF16)
            update = jnp.dot(gated, wo_ref[m], preferred_element_type=F32)
            unit_done(row, unit // per, at, update)

        scores(0, s_even, 0)

        def pair(t, carry):
            unit = 2 * t
            scores(unit + 1, s_odd, 1, (s_even, p_even, 0))
            values(unit, p_even)

            @pl.when(t == per // 2 - 1)
            def _():
                between()

            @pl.when(t < per - 1)
            def _():
                scores(unit + 2, s_even, 0, (s_odd, p_odd, 1))
                values(unit + 1, p_odd)

            @pl.when(t == per - 1)
            def _():
                weights(s_odd, p_odd, 1)
                values(unit + 1, p_odd)

            return carry

        lax.fori_loop(0, per, pair, 0)

    lax.fori_loop(1, key_n, send_a1, 0)
    x1[:, col_slice(c)] = x_ref[pl.ds(c * per, per)]

    tile_f[...] = layer_norm(x_ref[...].astype(F32), gain_ref[0:1], shift_ref[0:1])

    def pick(m, k):
        return jnp.where(lane_k % KEYS == k, wr_s[m], jnp.zeros((LANES, LANES), BF16))

    acc = jnp.zeros((rows_t, LANES), F32)
    for k in range(0, cols_t, 2):
        left = jnp.concatenate([tile_f[:, k, :], tile_f[:, k + 1, :]], axis=1).astype(BF16)
        right = jnp.concatenate([pick(0, k), pick(0, k + 1)], axis=0)
        acc = acc + jnp.dot(left, right, preferred_element_type=F32)
    bias_a[y, core, z, xx] = acc.astype(BF16)

    def more(m, xs, lo, hi):
        def one(i, carry):
            prepare(m, xs, i)
            return carry

        lax.fori_loop(lo, hi, one, 0)

    def widen_one(h):
        def widen(g, carry):
            at = pl.ds(pl.multiple_of(g * LANES, LANES), LANES)
            masked = key_bias(g)
            for rr in range(h * row_n // 2, (h + 1) * row_n // 2):
                block = bias_a[rr // 2, rr % 2, g // x_n, lax.rem(g, x_n)].astype(F32)
                bias_s[rr * rows_t : (rr + 1) * rows_t, at] = block + masked
            return carry

        lax.fori_loop(0, key_n, widen, 0)

    moves = Gather(bias_a, ga_send, ga_recv, "yzx")
    moves.start_one()
    moves.start_two()
    lax.fori_loop(1, key_n, wait_a1, 0)
    more(0, x1, 0, 1)
    moves.start_three(0)
    moves.start_three(1)
    more(0, x1, 1, per)
    moves.pass_on(0)
    moves.finish(0)
    widen_one(0)

    def a2_copy(i, n, to, frm):
        return remote(
            as1.at[pl.ds(i, n), col_slice(to)], t2.at[pl.ds(frm * per + i, n)], a2_send.at[to], a2_recv.at[frm], (r, to)
        )

    def unit_one(i, h, at, update):
        keep = kept(h * half_t, rows_t * r + per * c + i, half_t)
        as1[i, at, :] = (x1[i, at, :].astype(F32) + keep * update).astype(BF16)

        def send(o, inner):
            to = h * (key_n // 2) + lax.rem(c + o, key_n // 2)

            @pl.when(to != c)
            def _():
                a2_copy(i, 1, to, c).start()

            return inner

        lax.fori_loop(0, key_n // 2, send, 0)

    def between_one():
        moves.pass_on(1)
        moves.finish(1)
        widen_one(1)

    attend(0, unit_one, between_one)
    t2[pl.ds(per * c, per)] = as1[:, col_slice(c)]
    moves.drain()

    def wait_a2(o, carry):
        to = lax.rem(c + o, key_n)
        a2_copy(0, per, to, c).wait_send()
        frm = lax.rem(c + key_n - o, key_n)
        copy = remote(
            as1.at[pl.ds(0, per), col_slice(c)], t2.at[pl.ds(frm * per, per)], a2_send.at[frm], a2_recv.at[frm], (r, frm)
        )
        copy.wait_recv()
        return carry

    lax.fori_loop(1, key_n, wait_a2, 0)

    tile_f[...] = t2[...].astype(F32)
    for j in range(cols_t):
        sb[j] = tile_f[:, j, :].astype(BF16)

    def b2_copy(o, to, frm):
        return remote(sb.at[pl.ds(to * per, per)], x2.at[:, row_slice(frm)], b2_send.at[o], b2_recv.at[o], (to, c))

    def send_b2(o, carry):
        b2_copy(o, lax.rem(r + o, row_n), r).start()
        return carry

    def wait_b2(o, carry):
        b2_copy(o, lax.rem(r + o, row_n), r).wait_send()
        frm = lax.rem(r + row_n - o, row_n)
        b2_copy(o, frm, frm).wait_recv()
        return carry

    tile_f[...] = layer_norm(tile_f[...], gain_ref[1:2], shift_ref[1:2])
    halves = rows_t // KEYS

    acc = jnp.zeros((rows_t, LANES), F32)
    for k in range(0, KEYS, 2):
        left = jnp.concatenate(
            [jnp.concatenate([tile_f[h * KEYS + kk] for h in range(halves)], axis=0) for kk in (k, k + 1)], axis=1
        ).astype(BF16)
        right = jnp.concatenate([pick(1, k), pick(1, k + 1)], axis=0)
        acc = acc + jnp.dot(left, right, preferred_element_type=F32)
    bias_b[y, core, z, xx] = acc.astype(BF16)

    moves_two = Gather(bias_b, gb_send, gb_recv, "zyx")
    moves_two.start_one()
    lax.fori_loop(1, row_n, send_b2, 0)
    x2[:, row_slice(r)] = sb[pl.ds(r * per, per)]
    moves_two.start_two()
    lax.fori_loop(1, row_n, wait_b2, 0)
    more(1, x2, 0, 1)
    moves_two.start_three(0)
    moves_two.start_three(1)
    more(1, x2, 1, per)
    moves_two.pass_on(0)
    moves_two.finish(0)

    def widen_two(h):
        def widen(g, carry):
            for gg in range(row_n * halves):
                rr, hh = gg // halves, gg % halves
                block = bias_b[rr // 2, rr % 2, g // x_n, lax.rem(g, x_n), hh * KEYS : (hh + 1) * KEYS, :].astype(F32)
                bias_s[col_slice(g), gg * LANES : (gg + 1) * LANES] = block + key_bias(gg)
            return carry

        lax.fori_loop(h * key_n // 2, (h + 1) * key_n // 2, widen, 0)

    widen_two(0)

    def c2_copy(i, n, to, frm):
        return remote(
            np2.at[pl.ds(i, n), row_slice(to)], fin.at[pl.ds(frm * per + i, n)], c2_send.at[to], c2_recv.at[frm], (to, c)
        )

    def unit_two(i, h, at, update):
        keep = kept(h * half_t, cols_t * c + per * r + i, half_t)
        update = (keep * update).astype(BF16).astype(F32)
        np2[i, at, :] = (x2[i, at, :].astype(F32) + update).astype(BF16)

        def send(o, inner):
            to = h * (row_n // 2) + lax.rem(r + o, row_n // 2)

            @pl.when(to != r)
            def _():
                c2_copy(i, 1, to, r).start()

            return inner

        lax.fori_loop(0, row_n // 2, send, 0)

    def between_two():
        moves_two.pass_on(1)
        moves_two.finish(1)
        widen_two(1)

    attend(1, unit_two, between_two)
    fin[pl.ds(per * r, per)] = np2[:, row_slice(r)]
    moves_two.drain()

    def wait_c2(o, carry):
        c2_copy(0, per, lax.rem(r + o, row_n), r).wait_send()
        frm = lax.rem(r + row_n - o, row_n)
        copy = remote(
            np2.at[pl.ds(0, per), row_slice(r)], fin.at[pl.ds(frm * per, per)], c2_send.at[frm], c2_recv.at[frm], (frm, c)
        )
        copy.wait_recv()
        return carry

    lax.fori_loop(1, row_n, wait_c2, 0)
    for j in range(cols_t):
        tile_f[:, j, :] = fin[j].astype(F32)
    out_ref[...] = tile_f[...].astype(BF16)


def local(row_n, key_n, pair_rep, token_mask, norm_gain, norm_shift, w_proj, w_bias, gate_bias, w_out):
    rows_t, cols_t, channels = pair_rep.shape
    tokens = token_mask.shape[0]
    per = tokens // (row_n * key_n)
    groups = tokens // KEYS
    width = groups * LANES
    y_n, z_n = row_n // 2, int(round(key_n**0.5))
    slots = y_n - 1 + 2 * y_n * (z_n - 1) + y_n * z_n
    vmem, dma = pltpu.VMEM, pltpu.SemaphoreType.DMA
    buf = (y_n, 2, z_n, z_n, rows_t, LANES)
    return pl.pallas_call(
        functools.partial(kernel, tokens, row_n, key_n),
        out_shape=jax.ShapeDtypeStruct(pair_rep.shape, BF16),
        in_specs=[pl.BlockSpec(memory_space=pltpu.VMEM)] * 8,
        out_specs=pl.BlockSpec(memory_space=pltpu.VMEM),
        scratch_shapes=[
            vmem((per, tokens, LANES), BF16),
            vmem((per, tokens, LANES), BF16),
            vmem((per, tokens, LANES), BF16),
            vmem((per, tokens, LANES), BF16),
            vmem((rows_t, cols_t, LANES), BF16),
            vmem((cols_t, rows_t, LANES), BF16),
            vmem((cols_t, rows_t, LANES), BF16),
            vmem((rows_t, cols_t, LANES), F32),
            vmem(buf, BF16),
            vmem(buf, BF16),
            vmem((tokens, width), F32),
            vmem((per, tokens, LANES), BF16),
            vmem((per, width, LANES), BF16),
            vmem((per, width, 2 * LANES), BF16),
            vmem((per, tokens, LANES), F32),
            vmem((tokens // 2, width), F32),
            vmem((tokens // 2, width), F32),
            vmem((tokens // 2, width), BF16),
            vmem((tokens // 2, width), BF16),
            vmem((2, tokens // 2, LANES), F32),
            vmem((2, LANES, LANES), BF16),
            dma((key_n,)), dma((key_n,)), dma((key_n,)), dma((key_n,)),
            dma((row_n,)), dma((row_n,)), dma((row_n,)), dma((row_n,)),
            dma((slots,)), dma((slots,)), dma((slots,)), dma((slots,)),
        ],
        compiler_params=pltpu.CompilerParams(
            collective_id=0, has_side_effects=True, vmem_limit_bytes=56 * 2**20
        ),
        name="triangle_attention",
    )(
        pair_rep, token_mask.reshape(-1, min(tokens, LANES)), norm_gain, norm_shift, w_proj, w_bias, gate_bias, w_out,
    )


def solution(mesh):
    row_n, key_n = mesh.shape["rows"], mesh.shape["keys"]
    in_specs = (P("rows", "keys", None), P(), P(), P(), P(), P(), P(), P())
    out_specs = P("rows", "keys", None)
    return jax.shard_map(
        functools.partial(local, row_n, key_n), mesh=mesh, in_specs=in_specs, out_specs=out_specs, check_vma=False
    )
```

time: 101 us -> 81.2 us (0.80)
  Pallas kernels: 95.4 us -> 77.3 us
  local copies, waits for them, and re-layouts: 4.9 us -> 3.3 us
    pallas_call x1, Pallas kernels: 95.4 us -> 77.3 us  [local(): pl.pallas_call(functools.partial(kernel, tokens, row_n, key_n), out_shape...]
    unnamed x5 -> x2, local copies, waits for them, and re-layouts: 2.56 us -> 3.3 us
where the time goes in v2:
time: 81.2 us; the launch traced here: 80.6 us
  Pallas kernels  77.3 us (95%)
  local copies, waits for them, and re-layouts  3.3 us (4%)
    pallas_call x1, Pallas kernels, local(): pl.pallas_call(functools.partial(kernel, tokens, row_n, key_n), out_shape...  77.3 us
    unnamed x2, local copies, waits for them, and re-layouts  3.3 us

profile of v2, /device:TPU:1, one launch (start us, length us, event | category | flops | bytes accessed | tf_op | source)
XLA Modules:
  0.0 80.6 jit_solution(16689605155325425883)
XLA Ops:
  0.0 1.4 %copy.9.wb_ref = bf16[2,128,4]{2,1,0:T(8,128)(2,1)} copy(bf16[2,128,4]{1,2,0:T(4,128)(2,1)} %param.13) | data formatting | bytes 4096 | tf_op args[5]
  1.4 77.3 %triangle_attention.1 = bf16[64,32,128]{2,1,0:T(8,128)(2,1)} custom-call(bf16[64,32,128]{2,1,0:T(8,128)(2,1)} %x_ref.1, s32[4,128]{1,0:T(4,128)} %bitcast.1, f32[2,128]{1,0:T(2,128)} %gain_ref.1, f32[2,128]{1,0:T(2,128)} %shift_ref.1, bf16[2,128,512]{2,1,0:T(8,128)(2,1)} %wp_ref.1, bf16[2,128,4]{2,1,0:T(8,128)(2,1)} %copy.9.wb_ref, f32[2,128]{1,0:T(2,128)} %gb_ref.1, ...), custom_call_target="tpu_custom_call" | custom-call | tf_op jit(solution)/shard_map/triangle_attention/pallas_call | solution.py:508
  78.7 1.9 %copy.11 = bf16[64,32,128]{2,1,0:T(8,128)(2,1)} copy(bf16[64,32,128]{2,1,0:T(8,128)(2,1)} %triangle_attention.1) | data formatting | bytes 1048576

commit v3 on v2

--- a/solution.py
+++ b/solution.py
@@ -35,10 +35,10 @@
 
 def kernel(
     tokens, row_n, key_n,
-    x_ref, mask_ref, gain_ref, shift_ref, wp_ref, wb_ref, gb_ref, wo_ref,
-    out_ref,
-    x1, x2, as1, np2, t2, sb, fin, tile_f, bias_a, bias_b, bias_s, q_s, k_s, v_s, g_s,
-    s_even, s_odd, p_even, p_odd, top_s, wr_s,
+    x_hbm, mask_ref, gain_ref, shift_ref, wp_ref, wb_ref, gb_ref, wo_ref,
+    fin,
+    x1, x2, as1, np2, t2, sb, tile_f, bias_a, bias_b, bias_s, q_s, k_s, v_s, g_s,
+    s_even, s_odd, p_even, p_odd, top_s, wr_s, x_ref, x_sem,
     a1_send, a1_recv, a2_send, a2_recv, b2_send, b2_recv, c2_send, c2_recv,
     ga_send, ga_recv, gb_send, gb_recv,
 ):
@@ -54,6 +54,8 @@
     lane = lax.broadcasted_iota(jnp.int32, (1, LANES), 1)
 
     barrier = pltpu.get_barrier_semaphore()
+    x_copy = pltpu.make_async_copy(x_hbm, x_ref, x_sem)
+    x_copy.start()
 
     def greet_keys(o, carry):
         pl.semaphore_signal(barrier, inc=1, device_id=(r, lax.rem(c + o, key_n)), device_id_type=MESH)
@@ -89,7 +91,10 @@
     spread = lax.broadcasted_iota(jnp.int32, (HEADS, LANES), 0) == lax.broadcasted_iota(jnp.int32, (HEADS, LANES), 1) // KEYS
     spread = jnp.where(spread, 1.0, 0.0).astype(BF16)
     for m in range(2):
-        wr_s[m] = jnp.dot(wb_ref[m], spread, preferred_element_type=F32).astype(BF16)
+        wr_s[m] = lax.dot_general(
+            wb_ref[m], spread, (((0,), (0,)), ((), ())), preferred_element_type=F32
+        ).astype(BF16)
+    x_copy.wait()
     pl.semaphore_wait(barrier, key_n - 1 + row_n - 1)
 
     def remote(src, dst, send, recv, device):
@@ -490,9 +495,6 @@
         return carry
 
     lax.fori_loop(1, row_n, wait_c2, 0)
-    for j in range(cols_t):
-        tile_f[:, j, :] = fin[j].astype(F32)
-    out_ref[...] = tile_f[...].astype(BF16)
 
 
 def local(row_n, key_n, pair_rep, token_mask, norm_gain, norm_shift, w_proj, w_bias, gate_bias, w_out):
@@ -505,10 +507,10 @@
     slots = y_n - 1 + 2 * y_n * (z_n - 1) + y_n * z_n
     vmem, dma = pltpu.VMEM, pltpu.SemaphoreType.DMA
     buf = (y_n, 2, z_n, z_n, rows_t, LANES)
-    return pl.pallas_call(
+    turned = pl.pallas_call(
         functools.partial(kernel, tokens, row_n, key_n),
-        out_shape=jax.ShapeDtypeStruct(pair_rep.shape, BF16),
-        in_specs=[pl.BlockSpec(memory_space=pltpu.VMEM)] * 8,
+        out_shape=jax.ShapeDtypeStruct((cols_t, rows_t, channels), BF16),
+        in_specs=[pl.BlockSpec(memory_space=pl.ANY)] + [pl.BlockSpec(memory_space=pltpu.VMEM)] * 7,
         out_specs=pl.BlockSpec(memory_space=pltpu.VMEM),
         scratch_shapes=[
             vmem((per, tokens, LANES), BF16),
@@ -516,7 +518,6 @@
             vmem((per, tokens, LANES), BF16),
             vmem((per, tokens, LANES), BF16),
             vmem((rows_t, cols_t, LANES), BF16),
-            vmem((cols_t, rows_t, LANES), BF16),
             vmem((cols_t, rows_t, LANES), BF16),
             vmem((rows_t, cols_t, LANES), F32),
             vmem(buf, BF16),
@@ -532,6 +533,8 @@
             vmem((tokens // 2, width), BF16),
             vmem((2, tokens // 2, LANES), F32),
             vmem((2, LANES, LANES), BF16),
+            vmem((rows_t, cols_t, LANES), BF16),
+            dma,
             dma((key_n,)), dma((key_n,)), dma((key_n,)), dma((key_n,)),
             dma((row_n,)), dma((row_n,)), dma((row_n,)), dma((row_n,)),
             dma((slots,)), dma((slots,)), dma((slots,)), dma((slots,)),
@@ -541,8 +544,10 @@
         ),
         name="triangle_attention",
     )(
-        pair_rep, token_mask.reshape(-1, min(tokens, LANES)), norm_gain, norm_shift, w_proj, w_bias, gate_bias, w_out,
+        pair_rep, token_mask.reshape(-1, min(tokens, LANES)), norm_gain, norm_shift, w_proj, w_bias.transpose(0, 2, 1), gate_bias,
+        w_out,
     )
+    return turned.transpose(1, 0, 2)
 
 
 def solution(mesh):

time: 81.2 us -> 78.8 us (0.970)
  Pallas kernels: 77.3 us -> 76.1 us
  local copies, waits for them, and re-layouts: 3.3 us -> 2.18 us
    unnamed x2 -> x0, local copies, waits for them, and re-layouts: 3.3 us -> none
    transpose x0 -> x1, local copies, waits for them, and re-layouts: none -> 2.18 us  [local(): return turned.transpose(1, 0, 2)]
    pallas_call x1, Pallas kernels: 77.3 us -> 76.1 us  [local(): pl.pallas_call(functools.partial(kernel, tokens, row_n, key_n), out_shape...]
where the time goes in v3:
time: 78.8 us; the launch traced here: 78.3 us
  Pallas kernels  76.1 us (97%)
  local copies, waits for them, and re-layouts  2.18 us (3%)
    pallas_call x1, Pallas kernels, local(): pl.pallas_call(functools.partial(kernel, tokens, row_n, key_n), out_shape...  76.1 us
    transpose x1, local copies, waits for them, and re-layouts, local(): return turned.transpose(1, 0, 2)  2.18 us

profile of v3, /device:TPU:1, one launch (start us, length us, event | category | flops | bytes accessed | tf_op | source)
XLA Modules:
  0.0 78.3 jit_solution(16437622940130320721)
XLA Ops:
  0.0 76.1 %triangle_attention.1 = bf16[32,64,128]{2,1,0:T(8,128)(2,1)} custom-call(bf16[64,32,128]{2,1,0:T(8,128)(2,1)} %x_hbm.1, s32[4,128]{1,0:T(4,128)} %bitcast.4, f32[2,128]{1,0:T(2,128)} %gain_ref.1, f32[2,128]{1,0:T(2,128)} %shift_ref.1, bf16[2,128,512]{2,1,0:T(8,128)(2,1)} %wp_ref.1, bf16[2,4,128]{2,1,0:T(4,128)(2,1)} %bitcast.5, f32[2,128]{1,0:T(2,128)} %gb_ref.1, ...), custom_call_target="tpu_custom_call" | custom-call | tf_op jit(solution)/shard_map/triangle_attention/pallas_call | solution.py:510
  76.1 2.2 %copy.9 = bf16[64,32,128]{2,1,0:T(8,128)(2,1)} copy(bf16[64,32,128]{2,0,1:T(8,128)(2,1)} %bitcast.3) | data formatting | bytes 1048576 | tf_op jit(solution)/shard_map/transpose | solution.py:550

commit v4 on v3

--- a/solution.py
+++ b/solution.py
@@ -184,10 +184,15 @@
             for d in range(1, self.parts):
                 self.one(d, True).start()
 
-        def start_two(self):
+        def start_two(self, h):
             for d in range(1, self.parts):
-                self.one(d, False).wait_recv()
-            for p in range(self.parts):
+                near = shifted(self.first, self.parts - d)
+
+                @pl.when(near // (self.parts // 2) == h)
+                def _(d=d):
+                    self.one(d, False).wait_recv()
+
+            for p in self.half(h):
                 for d in self.steps():
                     self.two(p, d, True).start()
 
@@ -260,7 +265,7 @@
     def weight_chunk(s_s, p_s, n, top):
         p_s[:, n : n + CHUNK] = jnp.exp2((s_s[:, n : n + CHUNK] - top) * LOG2E).astype(BF16)
 
-    def attend(m, unit_done, between):
+    def attend(m, unit_done, hooks):
         units = 2 * per
 
         def where(unit):
@@ -294,12 +299,15 @@
 
         def pair(t, carry):
             unit = 2 * t
+
+            def run_hooks(odd):
+                for after, hook in hooks.items():
+                    if after % 2 == odd:
+                        pl.when(t == after // 2)(hook)
+
             scores(unit + 1, s_odd, 1, (s_even, p_even, 0))
             values(unit, p_even)
-
-            @pl.when(t == per // 2 - 1)
-            def _():
-                between()
+            run_hooks(0)
 
             @pl.when(t < per - 1)
             def _():
@@ -311,6 +319,7 @@
                 weights(s_odd, p_odd, 1)
                 values(unit + 1, p_odd)
 
+            run_hooks(1)
             return carry
 
         lax.fori_loop(0, per, pair, 0)
@@ -350,13 +359,14 @@
 
     moves = Gather(bias_a, ga_send, ga_recv, "yzx")
     moves.start_one()
-    moves.start_two()
+    moves.start_two(0)
     lax.fori_loop(1, key_n, wait_a1, 0)
     more(0, x1, 0, 1)
     moves.start_three(0)
-    moves.start_three(1)
+    moves.start_two(1)
     more(0, x1, 1, per)
     moves.pass_on(0)
+    moves.start_three(1)
     moves.finish(0)
     widen_one(0)
 
@@ -381,17 +391,14 @@
         lax.fori_loop(0, key_n // 2, send, 0)
 
     def between_one():
-        moves.pass_on(1)
         moves.finish(1)
         widen_one(1)
 
-    attend(0, unit_one, between_one)
-    t2[pl.ds(per * c, per)] = as1[:, col_slice(c)]
-    moves.drain()
+    def sent_a2(o, carry):
+        a2_copy(0, per, lax.rem(c + o, key_n), c).wait_send()
+        return carry
 
     def wait_a2(o, carry):
-        to = lax.rem(c + o, key_n)
-        a2_copy(0, per, to, c).wait_send()
         frm = lax.rem(c + key_n - o, key_n)
         copy = remote(
             as1.at[pl.ds(0, per), col_slice(c)], t2.at[pl.ds(frm * per, per)], a2_send.at[frm], a2_recv.at[frm], (r, frm)
@@ -399,48 +406,72 @@
         copy.wait_recv()
         return carry
 
-    lax.fori_loop(1, key_n, wait_a2, 0)
-
-    tile_f[...] = t2[...].astype(F32)
-    for j in range(cols_t):
-        sb[j] = tile_f[:, j, :].astype(BF16)
-
-    def b2_copy(o, to, frm):
-        return remote(sb.at[pl.ds(to * per, per)], x2.at[:, row_slice(frm)], b2_send.at[o], b2_recv.at[o], (to, c))
-
-    def send_b2(o, carry):
-        b2_copy(o, lax.rem(r + o, row_n), r).start()
-        return carry
-
-    def wait_b2(o, carry):
-        b2_copy(o, lax.rem(r + o, row_n), r).wait_send()
-        frm = lax.rem(r + row_n - o, row_n)
-        b2_copy(o, frm, frm).wait_recv()
-        return carry
-
-    tile_f[...] = layer_norm(tile_f[...], gain_ref[1:2], shift_ref[1:2])
+    moves_two = Gather(bias_b, gb_send, gb_recv, "zyx")
     halves = rows_t // KEYS
 
-    acc = jnp.zeros((rows_t, LANES), F32)
-    for k in range(0, KEYS, 2):
-        left = jnp.concatenate(
-            [jnp.concatenate([tile_f[h * KEYS + kk] for h in range(halves)], axis=0) for kk in (k, k + 1)], axis=1
-        ).astype(BF16)
-        right = jnp.concatenate([pick(1, k), pick(1, k + 1)], axis=0)
-        acc = acc + jnp.dot(left, right, preferred_element_type=F32)
-    bias_b[y, core, z, xx] = acc.astype(BF16)
-
-    moves_two = Gather(bias_b, gb_send, gb_recv, "zyx")
-    moves_two.start_one()
-    lax.fori_loop(1, row_n, send_b2, 0)
-    x2[:, row_slice(r)] = sb[pl.ds(r * per, per)]
-    moves_two.start_two()
-    lax.fori_loop(1, row_n, wait_b2, 0)
-    more(1, x2, 0, 1)
+    def b2_row(a, o, to):
+        return remote(sb.at[to * per + a], x2.at[a, row_slice(r)], b2_send.at[o], b2_recv.at[a], (to, c))
+
+    def b2_own(a):
+        return pltpu.make_async_copy(sb.at[r * per + a], x2.at[a, row_slice(r)], b2_recv.at[a])
+
+    def send_b2(a, carry):
+        def send(o, inner):
+            b2_row(a, o, lax.rem(r + o, row_n)).start()
+            return inner
+
+        lax.fori_loop(1, row_n, send, 0)
+        b2_own(a).start()
+        return carry
+
+    def wait_b2(a):
+        pltpu.make_async_copy(x2.at[a], x2.at[a], b2_recv.at[a]).wait()
+
+    def sent_b2(o, carry):
+        to = lax.rem(r + o, row_n)
+        rows_out = sb.at[pl.ds(to * per, per)]
+        remote(rows_out, rows_out, b2_send.at[o], b2_recv.at[0], (to, c)).wait_send()
+        return carry
+
+    def second_tile():
+        lax.fori_loop(1, key_n, wait_a2, 0)
+        t2[pl.ds(per * c, per)] = as1[:, col_slice(c)]
+        tile_f[...] = t2[...].astype(F32)
+        for j in range(cols_t):
+            sb[j] = tile_f[:, j, :].astype(BF16)
+        lax.fori_loop(0, per, send_b2, 0)
+        tile_f[...] = layer_norm(tile_f[...], gain_ref[1:2], shift_ref[1:2])
+        acc = jnp.zeros((rows_t, LANES), F32)
+        for k in range(0, KEYS, 2):
+            left = jnp.concatenate(
+                [jnp.concatenate([tile_f[h * KEYS + kk] for h in range(halves)], axis=0) for kk in (k, k + 1)], axis=1
+            ).astype(BF16)
+            right = jnp.concatenate([pick(1, k), pick(1, k + 1)], axis=0)
+            acc = acc + jnp.dot(left, right, preferred_element_type=F32)
+        bias_b[y, core, z, xx] = acc.astype(BF16)
+        moves_two.start_one()
+
+    early = z < z_n // 2
+
+    def early_tile():
+        pl.when(early)(second_tile)
+
+    attend(0, unit_one, {per - 3: lambda: moves.pass_on(1), per - 2: between_one, per + 1: early_tile})
+    moves_two.start_two(0)
+    pl.when(jnp.logical_not(early))(second_tile)
     moves_two.start_three(0)
+    wait_b2(0)
+    prepare(1, x2, 0)
+    moves_two.start_two(1)
+
+    def late_row(a, carry):
+        wait_b2(a)
+        prepare(1, x2, a)
+        return carry
+
+    lax.fori_loop(1, per, late_row, 0)
+    moves_two.pass_on(0)
     moves_two.start_three(1)
-    more(1, x2, 1, per)
-    moves_two.pass_on(0)
     moves_two.finish(0)
 
     def widen_two(h):
@@ -477,13 +508,15 @@
         lax.fori_loop(0, row_n // 2, send, 0)
 
     def between_two():
-        moves_two.pass_on(1)
         moves_two.finish(1)
         widen_two(1)
 
-    attend(1, unit_two, between_two)
+    attend(1, unit_two, {per - 3: lambda: moves_two.pass_on(1), per - 2: between_two})
     fin[pl.ds(per * r, per)] = np2[:, row_slice(r)]
+    moves.drain()
     moves_two.drain()
+    lax.fori_loop(1, key_n, sent_a2, 0)
+    lax.fori_loop(1, row_n, sent_b2, 0)
 
     def wait_c2(o, carry):
         c2_copy(0, per, lax.rem(r + o, row_n), r).wait_send()

time: 78.8 us -> 77.4 us (0.982)
  Pallas kernels: 76.1 us -> 75 us
    pallas_call x1, Pallas kernels: 76.1 us -> 75 us  [local(): pl.pallas_call(functools.partial(kernel, tokens, row_n, key_n), out_shape...]
where the time goes in v4:
time: 77.4 us; the launch traced here: 77.2 us
  Pallas kernels  75 us (97%)
  local copies, waits for them, and re-layouts  2.18 us (3%)
    pallas_call x1, Pallas kernels, local(): pl.pallas_call(functools.partial(kernel, tokens, row_n, key_n), out_shape...  75 us
    transpose x1, local copies, waits for them, and re-layouts, local(): return turned.transpose(1, 0, 2)  2.18 us

profile of v4, /device:TPU:1, one launch (start us, length us, event | category | flops | bytes accessed | tf_op | source)
XLA Modules:
  0.0 77.2 jit_solution(5772235235831588691)
XLA Ops:
  0.0 75.0 %triangle_attention.1 = bf16[32,64,128]{2,1,0:T(8,128)(2,1)} custom-call(bf16[64,32,128]{2,1,0:T(8,128)(2,1)} %x_hbm.1, s32[4,128]{1,0:T(4,128)} %bitcast.4, f32[2,128]{1,0:T(2,128)} %gain_ref.1, f32[2,128]{1,0:T(2,128)} %shift_ref.1, bf16[2,128,512]{2,1,0:T(8,128)(2,1)} %wp_ref.1, bf16[2,4,128]{2,1,0:T(4,128)(2,1)} %bitcast.5, f32[2,128]{1,0:T(2,128)} %gb_ref.1, ...), custom_call_target="tpu_custom_call" | custom-call | tf_op jit(solution)/shard_map/triangle_attention/pallas_call | solution.py:543
  75.0 2.2 %copy.9 = bf16[64,32,128]{2,1,0:T(8,128)(2,1)} copy(bf16[64,32,128]{2,0,1:T(8,128)(2,1)} %bitcast.3) | data formatting | bytes 1048576 | tf_op jit(solution)/shard_map/transpose | solution.py:583

commit v5 on v4

--- a/solution.py
+++ b/solution.py
@@ -35,10 +35,10 @@
 
 def kernel(
     tokens, row_n, key_n,
-    x_hbm, mask_ref, gain_ref, shift_ref, wp_ref, wb_ref, gb_ref, wo_ref,
+    x_hbm, mask_ref, gain_ref, shift_ref, wp_hbm, wb_ref, gb_ref, wo_hbm,
     fin,
     x1, x2, as1, np2, t2, sb, tile_f, bias_a, bias_b, bias_s, q_s, k_s, v_s, g_s,
-    s_even, s_odd, p_even, p_odd, top_s, wr_s, x_ref, x_sem,
+    s_even, s_odd, p_even, p_odd, top_s, wr_s, x_ref, wp_ref, wo_ref, x_sem,
     a1_send, a1_recv, a2_send, a2_recv, b2_send, b2_recv, c2_send, c2_recv,
     ga_send, ga_recv, gb_send, gb_recv,
 ):
@@ -54,8 +54,14 @@
     lane = lax.broadcasted_iota(jnp.int32, (1, LANES), 1)
 
     barrier = pltpu.get_barrier_semaphore()
-    x_copy = pltpu.make_async_copy(x_hbm, x_ref, x_sem)
+    x_copy = pltpu.make_async_copy(x_hbm, x_ref, x_sem.at[0])
     x_copy.start()
+    w_copies = (
+        pltpu.make_async_copy(wp_hbm, wp_ref, x_sem.at[1]),
+        pltpu.make_async_copy(wo_hbm, wo_ref, x_sem.at[2]),
+    )
+    for copy in w_copies:
+        copy.start()
 
     def greet_keys(o, carry):
         pl.semaphore_signal(barrier, inc=1, device_id=(r, lax.rem(c + o, key_n)), device_id_type=MESH)
@@ -87,15 +93,12 @@
             v_s[i, g * LANES : (g + 1) * LANES, LANES:] = ones
         return carry
 
-    lax.fori_loop(0, per, put_ones, 0)
     spread = lax.broadcasted_iota(jnp.int32, (HEADS, LANES), 0) == lax.broadcasted_iota(jnp.int32, (HEADS, LANES), 1) // KEYS
     spread = jnp.where(spread, 1.0, 0.0).astype(BF16)
     for m in range(2):
         wr_s[m] = lax.dot_general(
             wb_ref[m], spread, (((0,), (0,)), ((), ())), preferred_element_type=F32
         ).astype(BF16)
-    x_copy.wait()
-    pl.semaphore_wait(barrier, key_n - 1 + row_n - 1)
 
     def remote(src, dst, send, recv, device):
         return pltpu.make_async_remote_copy(
@@ -324,9 +327,7 @@
 
         lax.fori_loop(0, per, pair, 0)
 
-    lax.fori_loop(1, key_n, send_a1, 0)
-    x1[:, col_slice(c)] = x_ref[pl.ds(c * per, per)]
-
+    x_copy.wait()
     tile_f[...] = layer_norm(x_ref[...].astype(F32), gain_ref[0:1], shift_ref[0:1])
 
     def pick(m, k):
@@ -338,6 +339,7 @@
         right = jnp.concatenate([pick(0, k), pick(0, k + 1)], axis=0)
         acc = acc + jnp.dot(left, right, preferred_element_type=F32)
     bias_a[y, core, z, xx] = acc.astype(BF16)
+    pl.semaphore_wait(barrier, key_n - 1 + row_n - 1)
 
     def more(m, xs, lo, hi):
         def one(i, carry):
@@ -359,12 +361,16 @@
 
     moves = Gather(bias_a, ga_send, ga_recv, "yzx")
     moves.start_one()
+    lax.fori_loop(1, key_n, send_a1, 0)
+    x1[:, col_slice(c)] = x_ref[pl.ds(c * per, per)]
+    lax.fori_loop(0, per, put_ones, 0)
+    for copy in w_copies:
+        copy.wait()
     moves.start_two(0)
+    moves.start_three(0)
     lax.fori_loop(1, key_n, wait_a1, 0)
-    more(0, x1, 0, 1)
-    moves.start_three(0)
     moves.start_two(1)
-    more(0, x1, 1, per)
+    more(0, x1, 0, per)
     moves.pass_on(0)
     moves.start_three(1)
     moves.finish(0)
@@ -433,14 +439,12 @@
         remote(rows_out, rows_out, b2_send.at[o], b2_recv.at[0], (to, c)).wait_send()
         return carry
 
-    def second_tile():
+    def second_whole():
         lax.fori_loop(1, key_n, wait_a2, 0)
         t2[pl.ds(per * c, per)] = as1[:, col_slice(c)]
-        tile_f[...] = t2[...].astype(F32)
-        for j in range(cols_t):
-            sb[j] = tile_f[:, j, :].astype(BF16)
-        lax.fori_loop(0, per, send_b2, 0)
-        tile_f[...] = layer_norm(tile_f[...], gain_ref[1:2], shift_ref[1:2])
+
+    def second_bias():
+        tile_f[...] = layer_norm(t2[...].astype(F32), gain_ref[1:2], shift_ref[1:2])
         acc = jnp.zeros((rows_t, LANES), F32)
         for k in range(0, KEYS, 2):
             left = jnp.concatenate(
@@ -452,13 +456,22 @@
         moves_two.start_one()
 
     early = z < z_n // 2
-
-    def early_tile():
-        pl.when(early)(second_tile)
-
-    attend(0, unit_one, {per - 3: lambda: moves.pass_on(1), per - 2: between_one, per + 1: early_tile})
+    late = jnp.logical_not(early)
+
+    def early_bias():
+        @pl.when(early)
+        def _():
+            second_whole()
+            second_bias()
+
+    attend(0, unit_one, {per - 3: lambda: moves.pass_on(1), per - 2: between_one, 2 * per - 2: early_bias})
+    pl.when(late)(second_whole)
+    tile_f[...] = t2[...].astype(F32)
+    for j in range(cols_t):
+        sb[j] = tile_f[:, j, :].astype(BF16)
+    lax.fori_loop(0, per, send_b2, 0)
     moves_two.start_two(0)
-    pl.when(jnp.logical_not(early))(second_tile)
+    pl.when(late)(second_bias)
     moves_two.start_three(0)
     wait_b2(0)
     prepare(1, x2, 0)
@@ -543,7 +556,7 @@
     turned = pl.pallas_call(
         functools.partial(kernel, tokens, row_n, key_n),
         out_shape=jax.ShapeDtypeStruct((cols_t, rows_t, channels), BF16),
-        in_specs=[pl.BlockSpec(memory_space=pl.ANY)] + [pl.BlockSpec(memory_space=pltpu.VMEM)] * 7,
+        in_specs=[pl.BlockSpec(memory_space=pl.ANY if i in (0, 4, 7) else pltpu.VMEM) for i in range(8)],
         out_specs=pl.BlockSpec(memory_space=pltpu.VMEM),
         scratch_shapes=[
             vmem((per, tokens, LANES), BF16),
@@ -567,7 +580,9 @@
             vmem((2, tokens // 2, LANES), F32),
             vmem((2, LANES, LANES), BF16),
             vmem((rows_t, cols_t, LANES), BF16),
-            dma,
+            vmem(w_proj.shape, BF16),
+            vmem(w_out.shape, BF16),
+            dma((3,)),
             dma((key_n,)), dma((key_n,)), dma((key_n,)), dma((key_n,)),
             dma((row_n,)), dma((row_n,)), dma((row_n,)), dma((row_n,)),
             dma((slots,)), dma((slots,)), dma((slots,)), dma((slots,)),

time: 77.4 us -> 76.1 us (0.983)
  the two profiles are of different devices: /device:TPU:1 before, /device:TPU:121 now
where the time goes in v5:
time: 76.1 us; the launch traced here: 76 us
  Pallas kernels  73.8 us (97%)
  local copies, waits for them, and re-layouts  2.18 us (3%)
    pallas_call x1, Pallas kernels, local(): pl.pallas_call(functools.partial(kernel, tokens, row_n, key_n), out_shape...  73.8 us
    transpose x1, local copies, waits for them, and re-layouts, local(): return turned.transpose(1, 0, 2)  2.18 us

profile of v5, /device:TPU:121, one launch (start us, length us, event | category | flops | bytes accessed | tf_op | source)
XLA Modules:
  0.0 76.0 jit_solution(8921978063802949193)
XLA Ops:
  0.0 73.8 %triangle_attention.1 = bf16[32,64,128]{2,1,0:T(8,128)(2,1)} custom-call(bf16[64,32,128]{2,1,0:T(8,128)(2,1)} %x_hbm.1, s32[4,128]{1,0:T(4,128)} %bitcast.4, f32[2,128]{1,0:T(2,128)} %gain_ref.1, f32[2,128]{1,0:T(2,128)} %shift_ref.1, bf16[2,128,512]{2,1,0:T(8,128)(2,1)} %wp_hbm.1, bf16[2,4,128]{2,1,0:T(4,128)(2,1)} %bitcast.5, f32[2,128]{1,0:T(2,128)} %gb_ref.1, ...), custom_call_target="tpu_custom_call" | custom-call | tf_op jit(solution)/shard_map/triangle_attention/pallas_call | solution.py:556
  73.8 2.2 %copy.9 = bf16[64,32,128]{2,1,0:T(8,128)(2,1)} copy(bf16[64,32,128]{2,0,1:T(8,128)(2,1)} %bitcast.3) | data formatting | bytes 1048576 | tf_op jit(solution)/shard_map/transpose | solution.py:598

commit v6 on v5

--- a/solution.py
+++ b/solution.py
@@ -74,6 +74,20 @@
     lax.fori_loop(1, key_n, greet_keys, 0)
     lax.fori_loop(1, row_n, greet_rows, 0)
 
+    def greet_planes(o, carry):
+        far = lax.rem(y + 1 + o // (z_n - 1), y_n) * 2 + core
+        step = 1 + o % (z_n - 1)
+        pl.semaphore_signal(
+            barrier, inc=1, device_id=(far, lax.rem(z + step, z_n) * x_n + xx), device_id_type=MESH
+        )
+        pl.semaphore_signal(
+            barrier, inc=1, device_id=(far, z * x_n + lax.rem(xx + step, x_n)), device_id_type=MESH
+        )
+        return carry
+
+    planes = (y_n - 1) * (z_n - 1)
+    lax.fori_loop(0, planes, greet_planes, 0)
+
     real = jnp.sum(mask_ref[...], keepdims=True)
 
     def key_bias(g):
@@ -152,23 +166,31 @@
             u, v = self.others if p % 2 == 0 else self.others[::-1]
             return self.block(which_core, **{self.first: p, u: slice(None), v: at.get("v", place[v])})
 
-        def one(self, d, out):
-            near = shifted(self.first, size[self.first] - d)
-            if out:
-                return self.copy(d - 1, self.block(core), device(core, **{self.first: shifted(self.first, d)}))
-            return self.copy(d - 1, self.block(core, **{self.first: near}), device(core, **{self.first: near}))
-
-        def two(self, p, d, out):
+        def one(self, o):
+            first, (a, b) = self.first, self.others
+            odd = place[first] % 2
+            n = self.turns + 1
+            at = {
+                first: lax.rem(place[first] + o // n, self.parts),
+                a: lax.rem(place[a] + (o % n) * (1 - odd), size[a]),
+                b: lax.rem(place[b] + (o % n) * odd, size[b]),
+            }
+            return self.copy(o - 1, self.block(core), device(core, **at))
+
+        def wait_one(self, p):
             u = self.others[p % 2]
-            slot = self.parts - 1 + p * self.turns + d - 1
-            near = shifted(u, size[u] - d)
-            if out:
-                return self.copy(slot, self.block(core, **{self.first: p}), device(core, **{u: shifted(u, d)}))
-            return self.copy(slot, self.block(core, **{self.first: p, u: near}), device(core, **{u: near}))
+            away = lax.rem(place[self.first] + self.parts - p, self.parts)
+            for d in range(self.turns + 1):
+                at = {self.first: p, u: shifted(u, size[u] - d)}
+                arrived = self.copy(away * (self.turns + 1) + d - 1, self.block(core, **at), device(core, **at))
+                if d:
+                    arrived.wait_recv()
+                else:
+                    pl.when(away != 0)(arrived.wait_recv)
 
         def three(self, p, d, out):
             v = self.others[1 - p % 2]
-            slot = self.parts - 1 + (self.parts + p) * self.turns + d - 1
+            slot = self.parts * (self.turns + 1) - 1 + p * self.turns + d - 1
             near = shifted(v, size[v] - d)
             if out:
                 return self.copy(slot, self.line(p, core), device(core, **{v: shifted(v, d)}))
@@ -176,7 +198,7 @@
 
         def mate(self, p, d, out):
             v = self.others[1 - p % 2]
-            slot = self.parts - 1 + 2 * self.parts * self.turns + p * (self.turns + 1) + d
+            slot = self.parts * (self.turns + 1) - 1 + self.parts * self.turns + p * (self.turns + 1) + d
             near = shifted(v, size[v] - d)
             return self.copy(slot, self.line(p, core if out else 1 - core, v=near), device(1 - core))
 
@@ -184,28 +206,18 @@
             return range(1, self.turns + 1)
 
         def start_one(self):
-            for d in range(1, self.parts):
-                self.one(d, True).start()
-
-        def start_two(self, h):
-            for d in range(1, self.parts):
-                near = shifted(self.first, self.parts - d)
-
-                @pl.when(near // (self.parts // 2) == h)
-                def _(d=d):
-                    self.one(d, False).wait_recv()
-
-            for p in self.half(h):
-                for d in self.steps():
-                    self.two(p, d, True).start()
+            def send(o, carry):
+                self.one(o).start()
+                return carry
+
+            lax.fori_loop(1, self.parts * (self.turns + 1), send, 0)
 
         def half(self, h):
             return range(h * self.parts // 2, (h + 1) * self.parts // 2)
 
         def start_three(self, h):
             for p in self.half(h):
-                for d in self.steps():
-                    self.two(p, d, False).wait_recv()
+                self.wait_one(p)
                 for d in self.steps():
                     self.three(p, d, True).start()
                 self.mate(p, 0, True).start()
@@ -222,11 +234,13 @@
                     self.mate(p, d, False).wait_recv()
 
         def drain(self):
-            for d in range(1, self.parts):
-                self.one(d, True).wait_send()
+            def sent(o, carry):
+                self.one(o).wait_send()
+                return carry
+
+            lax.fori_loop(1, self.parts * (self.turns + 1), sent, 0)
             for p in range(self.parts):
                 for d in self.steps():
-                    self.two(p, d, True).wait_send()
                     self.three(p, d, True).wait_send()
                 for d in range(self.turns + 1):
                     self.mate(p, d, True).wait_send()
@@ -339,7 +353,7 @@
         right = jnp.concatenate([pick(0, k), pick(0, k + 1)], axis=0)
         acc = acc + jnp.dot(left, right, preferred_element_type=F32)
     bias_a[y, core, z, xx] = acc.astype(BF16)
-    pl.semaphore_wait(barrier, key_n - 1 + row_n - 1)
+    pl.semaphore_wait(barrier, key_n - 1 + row_n - 1 + 2 * planes)
 
     def more(m, xs, lo, hi):
         def one(i, carry):
@@ -366,13 +380,12 @@
     lax.fori_loop(0, per, put_ones, 0)
     for copy in w_copies:
         copy.wait()
-    moves.start_two(0)
     moves.start_three(0)
     lax.fori_loop(1, key_n, wait_a1, 0)
-    moves.start_two(1)
-    more(0, x1, 0, per)
+    more(0, x1, 0, 1)
+    moves.start_three(1)
+    more(0, x1, 1, per)
     moves.pass_on(0)
-    moves.start_three(1)
     moves.finish(0)
     widen_one(0)
 
@@ -465,26 +478,28 @@
             second_bias()
 
     attend(0, unit_one, {per - 3: lambda: moves.pass_on(1), per - 2: between_one, 2 * per - 2: early_bias})
-    pl.when(late)(second_whole)
+    moves_two.start_three(0)
+    @pl.when(late)
+    def _():
+        second_whole()
+        second_bias()
+
     tile_f[...] = t2[...].astype(F32)
     for j in range(cols_t):
         sb[j] = tile_f[:, j, :].astype(BF16)
     lax.fori_loop(0, per, send_b2, 0)
-    moves_two.start_two(0)
-    pl.when(late)(second_bias)
-    moves_two.start_three(0)
-    wait_b2(0)
-    prepare(1, x2, 0)
-    moves_two.start_two(1)
+    moves_two.pass_on(0)
+    moves.drain()
+    lax.fori_loop(1, key_n, sent_a2, 0)
 
     def late_row(a, carry):
         wait_b2(a)
         prepare(1, x2, a)
         return carry
 
+    lax.fori_loop(0, 1, late_row, 0)
+    moves_two.start_three(1)
     lax.fori_loop(1, per, late_row, 0)
-    moves_two.pass_on(0)
-    moves_two.start_three(1)
     moves_two.finish(0)
 
     def widen_two(h):
@@ -526,9 +541,7 @@
 
     attend(1, unit_two, {per - 3: lambda: moves_two.pass_on(1), per - 2: between_two})
     fin[pl.ds(per * r, per)] = np2[:, row_slice(r)]
-    moves.drain()
     moves_two.drain()
-    lax.fori_loop(1, key_n, sent_a2, 0)
     lax.fori_loop(1, row_n, sent_b2, 0)
 
     def wait_c2(o, carry):

time: 76.1 us -> 74.4 us (0.978)
  the two profiles are of different devices: /device:TPU:121 before, /device:TPU:1 now
where the time goes in v6:
time: 74.4 us; the launch traced here: 73.9 us
  Pallas kernels  71.8 us (97%)
  local copies, waits for them, and re-layouts  2.18 us (3%)
    pallas_call x1, Pallas kernels, local(): pl.pallas_call(functools.partial(kernel, tokens, row_n, key_n), out_shape...  71.8 us
    transpose x1, local copies, waits for them, and re-layouts, local(): return turned.transpose(1, 0, 2)  2.18 us

profile of v6, /device:TPU:1, one launch (start us, length us, event | category | flops | bytes accessed | tf_op | source)
XLA Modules:
  0.0 73.9 jit_solution(1297865520383904191)
XLA Ops:
  0.0 71.8 %triangle_attention.1 = bf16[32,64,128]{2,1,0:T(8,128)(2,1)} custom-call(bf16[64,32,128]{2,1,0:T(8,128)(2,1)} %x_hbm.1, s32[4,128]{1,0:T(4,128)} %bitcast.4, f32[2,128]{1,0:T(2,128)} %gain_ref.1, f32[2,128]{1,0:T(2,128)} %shift_ref.1, bf16[2,128,512]{2,1,0:T(8,128)(2,1)} %wp_hbm.1, bf16[2,4,128]{2,1,0:T(4,128)(2,1)} %bitcast.5, f32[2,128]{1,0:T(2,128)} %gb_ref.1, ...), custom_call_target="tpu_custom_call" | custom-call | tf_op jit(solution)/shard_map/triangle_attention/pallas_call | solution.py:569
  71.8 2.2 %copy.9 = bf16[64,32,128]{2,1,0:T(8,128)(2,1)} copy(bf16[64,32,128]{2,0,1:T(8,128)(2,1)} %bitcast.3) | data formatting | bytes 1048576 | tf_op jit(solution)/shard_map/transpose | solution.py:611

commit v7 on v6

--- a/solution.py
+++ b/solution.py
@@ -26,11 +26,12 @@
 
 
 def head_max(m, lane):
-    for step in (16, 8, 4, 2, 1):
-        below = pltpu.roll(m, step, 1)
-        above = pltpu.roll(m, LANES - step, 1)
-        m = jnp.maximum(m, jnp.where((lane & step) != 0, below, above))
-    return m
+    out = None
+    for h in range(HEADS):
+        mine = lane // KEYS == h
+        largest = jnp.max(jnp.where(mine, m, -jnp.inf), axis=-1, keepdims=True)
+        out = largest if out is None else jnp.where(mine, largest, out)
+    return jnp.broadcast_to(out, m.shape)
 
 
 def kernel(
@@ -203,7 +204,7 @@
             return self.copy(slot, self.line(p, core if out else 1 - core, v=near), device(1 - core))
 
         def steps(self):
-            return range(1, self.turns + 1)
+            return sorted(range(1, self.turns + 1), key=lambda d: min(d, self.turns + 1 - d))
 
         def start_one(self):
             def send(o, carry):

time: 74.4 us -> 72.8 us (0.978)
  Pallas kernels: 71.8 us -> 70.4 us
    pallas_call x1, Pallas kernels: 71.8 us -> 70.4 us  [local(): pl.pallas_call(functools.partial(kernel, tokens, row_n, key_n), out_shape...]
where the time goes in v7:
time: 72.8 us; the launch traced here: 72.6 us
  Pallas kernels  70.4 us (97%)
  local copies, waits for them, and re-layouts  2.18 us (3%)
    pallas_call x1, Pallas kernels, local(): pl.pallas_call(functools.partial(kernel, tokens, row_n, key_n), out_shape...  70.4 us
    transpose x1, local copies, waits for them, and re-layouts, local(): return turned.transpose(1, 0, 2)  2.18 us

profile of v7, /device:TPU:1, one launch (start us, length us, event | category | flops | bytes accessed | tf_op | source)
XLA Modules:
  0.0 72.6 jit_solution(9085783622264946120)
XLA Ops:
  0.0 70.4 %triangle_attention.1 = bf16[32,64,128]{2,1,0:T(8,128)(2,1)} custom-call(bf16[64,32,128]{2,1,0:T(8,128)(2,1)} %x_hbm.1, s32[4,128]{1,0:T(4,128)} %bitcast.4, f32[2,128]{1,0:T(2,128)} %gain_ref.1, f32[2,128]{1,0:T(2,128)} %shift_ref.1, bf16[2,128,512]{2,1,0:T(8,128)(2,1)} %wp_hbm.1, bf16[2,4,128]{2,1,0:T(4,128)(2,1)} %bitcast.5, f32[2,128]{1,0:T(2,128)} %gb_ref.1, ...), custom_call_target="tpu_custom_call" | custom-call | tf_op jit(solution)/shard_map/triangle_attention/pallas_call | solution.py:570
  70.4 2.2 %copy.9 = bf16[64,32,128]{2,1,0:T(8,128)(2,1)} copy(bf16[64,32,128]{2,0,1:T(8,128)(2,1)} %bitcast.3) | data formatting | bytes 1048576 | tf_op jit(solution)/shard_map/transpose | solution.py:612

commit v8 on v7

--- a/solution.py
+++ b/solution.py
@@ -55,11 +55,18 @@
     lane = lax.broadcasted_iota(jnp.int32, (1, LANES), 1)
 
     barrier = pltpu.get_barrier_semaphore()
-    x_copy = pltpu.make_async_copy(x_hbm, x_ref, x_sem.at[0])
-    x_copy.start()
+    piece = rows_t // 4
+    x_copies = [
+        pltpu.make_async_copy(
+            x_hbm.at[i * piece : (i + 1) * piece], x_ref.at[i * piece : (i + 1) * piece], x_sem.at[2 + i]
+        )
+        for i in range(4)
+    ]
+    for copy in x_copies:
+        copy.start()
     w_copies = (
-        pltpu.make_async_copy(wp_hbm, wp_ref, x_sem.at[1]),
-        pltpu.make_async_copy(wo_hbm, wo_ref, x_sem.at[2]),
+        pltpu.make_async_copy(wp_hbm, wp_ref, x_sem.at[0]),
+        pltpu.make_async_copy(wo_hbm, wo_ref, x_sem.at[1]),
     )
     for copy in w_copies:
         copy.start()
@@ -342,8 +349,10 @@
 
         lax.fori_loop(0, per, pair, 0)
 
-    x_copy.wait()
-    tile_f[...] = layer_norm(x_ref[...].astype(F32), gain_ref[0:1], shift_ref[0:1])
+    for i, copy in enumerate(x_copies):
+        copy.wait()
+        rows = slice(i * piece, (i + 1) * piece)
+        tile_f[rows] = layer_norm(x_ref[rows].astype(F32), gain_ref[0:1], shift_ref[0:1])
 
     def pick(m, k):
         return jnp.where(lane_k % KEYS == k, wr_s[m], jnp.zeros((LANES, LANES), BF16))
@@ -596,7 +605,7 @@
             vmem((rows_t, cols_t, LANES), BF16),
             vmem(w_proj.shape, BF16),
             vmem(w_out.shape, BF16),
-            dma((3,)),
+            dma((6,)),
             dma((key_n,)), dma((key_n,)), dma((key_n,)), dma((key_n,)),
             dma((row_n,)), dma((row_n,)), dma((row_n,)), dma((row_n,)),
             dma((slots,)), dma((slots,)), dma((slots,)), dma((slots,)),

time: 72.8 us -> 72.7 us (level)
  no operation moved by 1% of the time
where the time goes in v8:
time: 72.7 us; the launch traced here: 72.4 us
  Pallas kernels  70.2 us (97%)
  local copies, waits for them, and re-layouts  2.18 us (3%)
    pallas_call x1, Pallas kernels, local(): pl.pallas_call(functools.partial(kernel, tokens, row_n, key_n), out_shape...  70.2 us
    transpose x1, local copies, waits for them, and re-layouts, local(): return turned.transpose(1, 0, 2)  2.18 us

profile of v8, /device:TPU:1, one launch (start us, length us, event | category | flops | bytes accessed | tf_op | source)
XLA Modules:
  0.0 72.4 jit_solution(11597632171397470513)
XLA Ops:
  0.0 70.2 %triangle_attention.1 = bf16[32,64,128]{2,1,0:T(8,128)(2,1)} custom-call(bf16[64,32,128]{2,1,0:T(8,128)(2,1)} %x_hbm.1, s32[4,128]{1,0:T(4,128)} %bitcast.4, f32[2,128]{1,0:T(2,128)} %gain_ref.1, f32[2,128]{1,0:T(2,128)} %shift_ref.1, bf16[2,128,512]{2,1,0:T(8,128)(2,1)} %wp_hbm.1, bf16[2,4,128]{2,1,0:T(4,128)(2,1)} %bitcast.5, f32[2,128]{1,0:T(2,128)} %gb_ref.1, ...), custom_call_target="tpu_custom_call" | custom-call | tf_op jit(solution)/shard_map/triangle_attention/pallas_call | solution.py:579
  70.2 2.2 %copy.9 = bf16[64,32,128]{2,1,0:T(8,128)(2,1)} copy(bf16[64,32,128]{2,0,1:T(8,128)(2,1)} %bitcast.3) | data formatting | bytes 1048576 | tf_op jit(solution)/shard_map/transpose | solution.py:621
